TPU v7x, 128 devices: a whole 4x4x4 slice. The times are simulated.
128 devices in a mesh: grp: 4 (over y), dom: 32 (over x, z, core).
Axes of the slice: x: 4, y: 4, z: 4, core: 2. Of those that a mesh axis runs over, the one named last changes fastest.
Arguments:
- velocity: float32 [3, 64, 1024, 256], P(None, 'grp', 'dom'), may hold values from -6 to 6
- damping: float32 [64, 1024, 256], P('grp', 'dom'), may hold values from 0.02 to 0.5
- displacement: float32 [3, 524288], P(None, ('grp', 'dom')), may hold values from -6 to 6
- stiffness: float32 [12, 12, 524288], P(None, None, ('grp', 'dom'))
- connectivity: int32 [4, 524288], P(None, ('grp', 'dom')), may hold values from 0 to 4159, as said below
- inv_mass: float32 [524288], P(('grp', 'dom')), may hold values from 0.05 to 0.3
- iface_cell: int32 [16384], P(('grp', 'dom')), may hold values from 0 to 131071
- iface_owner: int32 [16384, 1], P(('grp', 'dom')), may hold values from 0 to 127; in each aligned block of 128 rows (0 to 127, 128 to 255, ...) at most 2 rows name the same one
- iface_node: int32 [16384], P(('grp', 'dom')), may hold values from 0 to 4092
- rbf_weight: float32 [4, 16384], P(None, ('grp', 'dom')), may hold values from 0.1 to 1
- normals: float32 [3, 16384], P(None, ('grp', 'dom')), may hold values from -6 to 6
Outputs:
- new_velocity: float32 [3, 64, 1024, 256], P(None, 'grp', 'dom')
- pressure: float32 [64, 1024, 256], P('grp', 'dom')
- new_displacement: float32 [3, 524288], P(None, ('grp', 'dom'))
- iface_velocity: float32 [3, 16384], P(None, ('grp', 'dom'))
Inputs may be any that keep to these rules, and one draw needn't show every extreme that they name: `connectivity`: the four corners of element e (e its local number on the device) are four different local nodes from e to e + 64, in no fixed order; numbers from 4096 on name the first 64 nodes of the next device along grp+dom. `iface_owner`: among the 128 points of one device, at most 2 have the same owner.
All inputs are finite; a program needn't handle non-finite values.
Results may differ from a plain program's by a relative error of at most 0.0001.
Values sent between devices are 32-bit elements; how exact they have to be, the bound alone decides.
A program may use at most 192 MiB of HBM per device.

v0:
```python
import jax
import jax.numpy as jnp
from jax import lax
from jax.sharding import PartitionSpec as P

ITERS = 4
RIM = 64
RBFW = 4


TIME_STEP = 0.1
VISCOSITY = 1.0
WALL_FRICTION = 0.5
SHELL_STEP = 0.5
UNIT_STEPS = ((1, 0, 0), (0, 1, 0), (0, 0, 1))


def with_halo(block, sides, width):
    for axis, dim in sides:
        count = lax.axis_size(axis)
        forward = [(i, i + 1) for i in range(count - 1)]
        backward = [(target, source) for source, target in forward]
        low = lax.ppermute(
            lax.slice_in_dim(block, block.shape[dim] - width, None, axis=dim), axis, forward
        )
        high = lax.ppermute(lax.slice_in_dim(block, 0, width, axis=dim), axis, backward)
        block = jnp.concatenate([low, block, high], axis=dim)
    return block


def from_behind(value, axis, steps):
    count = lax.axis_size(axis)
    leading, last = (max(0, -steps), min(count, count - steps))
    return lax.ppermute(value, axis, [(source, source + steps) for source in range(leading, last)])


def window_at(padded, offsets):
    size_x = padded.shape[-3] - 2
    size_y = padded.shape[-2] - 2
    size_z = padded.shape[-1] - 2
    return padded[
        ...,
        1 + offsets[0] : 1 + offsets[0] + size_x,
        1 + offsets[1] : 1 + offsets[1] + size_y,
        1 + offsets[2] : 1 + offsets[2] + size_z,
    ]


def backward(unit_step):
    return tuple((-value for value in unit_step))


def pad_depth(source):
    spec = [(0, 0)] * (source.ndim - 1) + [(1, 1)]
    return jnp.pad(source, spec)


def predictor(padded):
    centre = window_at(padded, (0, 0, 0))
    laplace = -6.0 * centre
    advect = jnp.zeros_like(centre)
    for axis_num, unit_step in enumerate(UNIT_STEPS):
        forward = window_at(padded, unit_step)
        behind_cells = window_at(padded, backward(unit_step))
        laplace = laplace + forward + behind_cells
        advect = advect + centre[axis_num : axis_num + 1] * (0.5 * (forward - behind_cells))
    return centre + TIME_STEP * (VISCOSITY * laplace - advect)


def divergence(padded):
    summed = jnp.zeros(window_at(padded[0], (0, 0, 0)).shape, jnp.float32)
    for axis_num, unit_step in enumerate(UNIT_STEPS):
        component = padded[axis_num]
        summed = summed + 0.5 * (
            window_at(component, unit_step) - window_at(component, backward(unit_step))
        )
    return -summed


def padded_cells(source):
    extended = with_halo(source, (("grp", 0), ("dom", 1)), 1)
    return pad_depth(extended)


def operate(source, damping):
    padded = padded_cells(source)
    centre = window_at(padded, (0, 0, 0))
    beside = jnp.zeros_like(centre)
    for unit_step in UNIT_STEPS:
        beside = beside + window_at(padded, unit_step) + window_at(padded, backward(unit_step))
    return (6.0 + damping) * centre - beside


def squares(residual):
    return lax.psum(jnp.sum(residual * residual), ("grp", "dom"))


def local(
    velocity,
    damping,
    displacement,
    stiffness,
    connectivity,
    inv_mass,
    iface_cell,
    iface_owner,
    iface_node,
    rbf_weight,
    normals,
):
    shell_nodes = displacement.shape[1]
    rim_values = from_behind(displacement[:, :RIM], ("grp", "dom"), -1)
    extended_disp = jnp.concatenate([displacement, rim_values], axis=1)
    element_count = connectivity.shape[1]
    corner_values = extended_disp[:, connectivity]
    element_dofs = jnp.transpose(corner_values, (1, 0, 2)).reshape(12, element_count)
    element_force = jnp.sum(stiffness * element_dofs[None], axis=1).reshape(4, 3, element_count)
    node_force = jnp.zeros((3, shell_nodes + RIM), jnp.float32)
    for corner in range(4):
        node_force = node_force.at[:, connectivity[corner]].add(element_force[corner])
    rim_force = from_behind(node_force[:, shell_nodes:], ("grp", "dom"), 1)
    stiff_force = node_force[:, :shell_nodes] + jnp.pad(rim_force, ((0, 0), (0, shell_nodes - RIM)))
    extended = with_halo(velocity, (("grp", 1), ("dom", 2)), 1)
    predicted = predictor(pad_depth(extended))
    star_wide = with_halo(predicted, (("grp", 1), ("dom", 2)), 1)
    star_padded = pad_depth(star_wide)
    right_side = divergence(star_padded)
    pressure = jnp.zeros_like(right_side)
    residual = right_side
    direction = right_side
    norm_now = squares(residual)
    for sweep in range(ITERS):
        mapped = operate(direction, damping)
        step_size = norm_now / lax.psum(jnp.sum(direction * mapped), ("grp", "dom"))
        pressure = pressure + step_size * direction
        residual = residual - step_size * mapped
        norm_next = squares(residual)
        direction = residual + norm_next / norm_now * direction
        norm_now = norm_next
    pressure_wide = padded_cells(pressure)
    new_velocity = predicted - jnp.stack(
        [
            0.5
            * (window_at(pressure_wide, unit_step) - window_at(pressure_wide, backward(unit_step)))
            for unit_step in UNIT_STEPS
        ]
    )
    pressure_at = pressure.reshape(-1)[iface_cell]
    velocity_at = new_velocity.reshape(3, -1)[:, iface_cell]
    traction = -pressure_at[None] * normals + WALL_FRICTION * velocity_at
    owner_dev = iface_owner[:, 0]
    point_count = owner_dev.shape[0]
    devices = lax.axis_size("grp") * lax.axis_size("dom")
    owner_cap = max(2, 2 * point_count // devices)
    order_index = lax.iota(jnp.int32, point_count)
    earlier = (owner_dev[None, :] == owner_dev[:, None]) & (
        order_index[None, :] < order_index[:, None]
    )
    slot_rank = jnp.sum(earlier.astype(jnp.int32), axis=1)
    slot_index = owner_dev * owner_cap + slot_rank
    slot_count = devices * owner_cap
    payload = jnp.concatenate([traction, rbf_weight, iface_node.astype(jnp.float32)[None]], axis=0)
    outgoing = jnp.zeros((payload.shape[0], slot_count), jnp.float32).at[:, slot_index].set(payload)
    received = lax.all_to_all(outgoing, ("grp", "dom"), split_axis=1, concat_axis=1, tiled=True)
    slot_traction = received[:3]
    slot_weight = received[3 : 3 + RBFW]
    slot_node = received[3 + RBFW].astype(jnp.int32)
    applied = jnp.zeros((3, shell_nodes), jnp.float32)
    for offset in range(RBFW):
        applied = applied.at[:, slot_node + offset].add(slot_weight[offset][None] * slot_traction)
    node_velocity = inv_mass[None] * (applied - stiff_force)
    new_displacement = displacement + SHELL_STEP * node_velocity
    slot_velocity = jnp.zeros((3, slot_count), jnp.float32)
    for offset in range(RBFW):
        slot_velocity = (
            slot_velocity + slot_weight[offset][None] * node_velocity[:, slot_node + offset]
        )
    returned_vals = lax.all_to_all(
        slot_velocity, ("grp", "dom"), split_axis=1, concat_axis=1, tiled=True
    )
    iface_velocity = returned_vals[:, slot_index]
    return (new_velocity, pressure, new_displacement, iface_velocity)


def solution(mesh):
    return jax.shard_map(
        local,
        mesh=mesh,
        in_specs=(
            P(None, "grp", "dom", None),
            P("grp", "dom", None),
            P(None, ("grp", "dom")),
            P(None, None, ("grp", "dom")),
            P(None, ("grp", "dom")),
            P(("grp", "dom")),
            P(("grp", "dom")),
            P(("grp", "dom"), None),
            P(("grp", "dom")),
            P(None, ("grp", "dom")),
            P(None, ("grp", "dom")),
        ),
        out_specs=(
            P(None, "grp", "dom", None),
            P("grp", "dom", None),
            P(None, ("grp", "dom")),
            P(None, ("grp", "dom")),
        ),
        check_vma=False,
    )
```

profile of v0, /device:TPU:1, one launch (start us, length us, event | category | flops | bytes accessed | tf_op | source)
XLA Modules:
  0.0 883.0 jit_solution(13403688143112464117)
XLA Ops:
  1.6 4.0 collective-permute-start.1
  11.1 4.0 collective-permute-start.2
  28.8 4.1 collective-permute-done.5
  33.0 5.3 collective-permute-start.6
  64.3 74.2 %all-reduce.8 = (f32[]{:T(128)}, f32[]{:T(128)}) all-reduce(f32[]{:T(128)} %get-tuple-element.33, f32[]{:T(128)} %get-tuple-element.32), channel_id=1, replica_groups=mesh['grp'=4,'dom'=32] {'grp','dom'}, use_global_device_ids=true, to_apply=%region_1.0 | all-reduce | flops 2 | bytes 16 | tf_op jit(solution)/shard_map/psum | solution.py:95
  141.6 63.6 %psum.58 = f32[]{:T(128)} all-reduce(f32[]{:T(128)} %multiply_reduce_fusion.5), channel_id=1, replica_groups=mesh['grp'=4,'dom'=32] {'grp','dom'}, use_global_device_ids=true, to_apply=%region_5.6 | all-reduce | flops 1 | bytes 8 | tf_op jit(solution)/shard_map/psum | solution.py:95
  223.4 66.3 %psum.59 = f32[]{:T(128)} all-reduce(f32[]{:T(128)} %get-tuple-element.46), channel_id=1, replica_groups=mesh['grp'=4,'dom'=32] {'grp','dom'}, use_global_device_ids=true, to_apply=%region_7.8 | all-reduce | flops 1 | bytes 8 | tf_op jit(solution)/shard_map/psum | solution.py:134
  293.8 62.9 %psum.60 = f32[]{:T(128)} all-reduce(f32[]{:T(128)} %get-tuple-element.44), channel_id=1, replica_groups=mesh['grp'=4,'dom'=32] {'grp','dom'}, use_global_device_ids=true, to_apply=%region_9.10 | all-reduce | flops 1 | bytes 8 | tf_op jit(solution)/shard_map/psum | solution.py:95
  375.0 66.8 %psum.61 = f32[]{:T(128)} all-reduce(f32[]{:T(128)} %get-tuple-element.42), channel_id=1, replica_groups=mesh['grp'=4,'dom'=32] {'grp','dom'}, use_global_device_ids=true, to_apply=%region_11.12 | all-reduce | flops 1 | bytes 8 | tf_op jit(solution)/shard_map/psum | solution.py:134
  445.1 62.5 %psum.62 = f32[]{:T(128)} all-reduce(f32[]{:T(128)} %multiply_reduce_fusion.1), channel_id=1, replica_groups=mesh['grp'=4,'dom'=32] {'grp','dom'}, use_global_device_ids=true, to_apply=%region_13.14 | all-reduce | flops 1 | bytes 8 | tf_op jit(solution)/shard_map/psum | solution.py:95
  527.8 66.8 %psum.63 = f32[]{:T(128)} all-reduce(f32[]{:T(128)} %fusion.18), channel_id=1, replica_groups=mesh['grp'=4,'dom'=32] {'grp','dom'}, use_global_device_ids=true, to_apply=%region_15.16 | all-reduce | flops 1 | bytes 8 | tf_op jit(solution)/shard_map/psum | solution.py:134
  605.4 56.0 %gather_fusion.2 = f32[16384,3]{1,0:T(8,128)} fusion(f32[3,4160]{0,1:T(8,128)} %copy.162, s32[16384]{0:T(1024)S(1)} %broadcast_clamp_fusion), kind=kCustom, calls=%fused_computation.2 | custom fusion | bytes 458752 | tf_op jit(solution)/shard_map/gather | solution.py:115
  661.4 5.4 copy.163
  678.0 32.4 %copy.154 = f32[3,16,32,256]{0,3,2,1:T(8,128)} copy(f32[3,16,32,256]{3,2,1,0:T(8,128)S(1)} %maximum_subtract_fusion) | data formatting | bytes 3145728 | tf_op jit(solution)/shard_map/sub | solution.py:141
  713.8 6.0 all-to-all-start
  727.7 23.2 %scatter_custom_fusion.5 = f32[3,4160]{0,1:T(8,128)S(1)} fusion(s32[4096]{0:T(1024)S(1)} %bitcast.107, f32[4096,3]{1,0:T(8,128)} %copy.164, f32[]{:T(128)} %constant.17.clone.1), kind=kCustom, calls=%fused_computation.63 | custom fusion | flops 12288 | bytes 50432 | tf_op jit(solution)/shard_map/scatter-add | solution.py:120
  750.9 23.5 %scatter_fusion.3 = f32[3,4160]{0,1:T(8,128)S(1)} fusion(f32[3,4160]{0,1:T(8,128)S(1)} %scatter_custom_fusion.5, s32[4096]{0:T(1024)S(1)} %bitcast.106, f32[4096,3]{1,0:T(8,128)} %copy.165), kind=kCustom, calls=%fused_computation.14 | custom fusion | flops 12288 | bytes 163840 | tf_op jit(solution)/shard_map/scatter-add | solution.py:120
  774.4 23.5 %scatter_fusion.4 = f32[3,4160]{0,1:T(8,128)S(1)} fusion(f32[3,4160]{0,1:T(8,128)S(1)} %scatter_fusion.3, s32[4096]{0:T(1024)S(1)} %bitcast.105, f32[4096,3]{1,0:T(8,128)} %copy.166), kind=kCustom, calls=%fused_computation.15 | custom fusion | flops 12288 | bytes 163840 | tf_op jit(solution)/shard_map/scatter-add | solution.py:120
  797.8 23.7 %scatter_fusion.5 = f32[3,4160]{0,1:T(8,128)S(1)} fusion(f32[3,4160]{0,1:T(8,128)S(1)} %scatter_fusion.4, s32[4096]{0:T(1024)S(1)} %bitcast.104, f32[4096,3]{1,0:T(8,128)} %copy.167), kind=kCustom, calls=%fused_computation.16 | custom fusion | flops 12288 | bytes 163840 | tf_op jit(solution)/shard_map/scatter-add | solution.py:120
  833.2 4.7 scatter_fusion
  837.8 4.6 scatter_fusion.1
  842.5 4.6 scatter_fusion.2
  862.5 9.2 %all-to-all-start.1 = ((f32[3,128,2]{0,2,1:T(2,128)}), f32[3,128,2]{0,2,1:T(2,128)S(1)}, u32[]{:S(2)}, u32[]{:S(2)}) async-start(f32[3,128,2]{0,2,1:T(2,128)} %multiply_add_fusion.6), calls=%async_computation.1 | async-start | bytes 262144 | tf_op jit(solution)/shard_map/all_to_all | solution.py:178
  873.0 8.5 all-to-all-done.1
  (199 shorter events, 166.0 us)
Async XLA Ops:
  1.6 5.7 collective-permute-start.1
  5.6 5.4 collective-permute-start
  11.1 7.7 collective-permute-start.2
  27.1 5.8 collective-permute-start.5
  33.0 7.2 collective-permute-start.6
  38.2 5.5 collective-permute-start.7
  47.8 5.4 collective-permute-start.8
  54.3 7.5 collective-permute-start.10
  56.2 5.6 collective-permute-start.11
  59.9 543.4 %collective-permute-start.28 = (f32[3,64]{1,0:T(4,128)S(1)}, f32[3,64]{1,0:T(4,128)S(1)}, u32[]{:S(2)}, u32[]{:S(2)}) collective-permute-start(f32[3,64]{1,0:T(4,128)S(1)} %slice.459), channel_id=1, source_target_pairs={{1,0},{2,1},{3,2},{4,3},{5,4},{6,5},{7,6},{8,7},{9,8},{10,9},{11,1... | collective-permute-start | bytes 2312 | tf_op jit(solution)/shard_map/ppermute | solution.py:34
  207.7 5.3 collective-permute-start.12
  214.1 5.9 collective-permute-start.14
  359.2 5.6 collective-permute-start.16
  360.7 5.0 collective-permute-start.17
  365.7 6.1 collective-permute-start.18
  510.4 5.5 collective-permute-start.20
  516.8 6.6 collective-permute-start.22
  598.0 68.9 %collective-permute-start.24 = (f32[1,32,256]{2,1,0:T(8,128)S(1)}, f32[1,32,256]{2,1,0:T(8,128)S(1)}, u32[]{:S(2)}, u32[]{:S(2)}) collective-permute-start(f32[1,32,256]{2,1,0:T(8,128)S(1)} %get-tuple-element.78), channel_id=1, source_target_pairs={{32,0},{64,32},{96,64},{33,1},{65,33},{97,65},{34,2},{66,34},{98,6... | collective-permute-start | bytes 98312 | tf_op jit(solution)/shard_map/ppermute | solution.py:26
  599.3 67.6 %collective-permute-start.25 = (f32[1,32,256]{2,1,0:T(8,128)S(1)}, f32[1,32,256]{2,1,0:T(8,128)S(1)}, u32[]{:S(2)}, u32[]{:S(2)}) collective-permute-start(f32[1,32,256]{2,1,0:T(8,128)S(1)} %get-tuple-element.77), channel_id=1, source_target_pairs={{0,32},{32,64},{64,96},{1,33},{33,65},{65,97},{2,34},{34,66},{66,9... | collective-permute-start | bytes 98312 | tf_op jit(solution)/shard_map/ppermute | solution.py:23
  666.9 9.8 %collective-permute-start.26 = (f32[18,1,256]{2,1,0:T(1,128)S(1)}, f32[18,1,256]{2,1,0:T(1,128)S(1)}, u32[]{:S(2)}, u32[]{:S(2)}) collective-permute-start(f32[18,1,256]{2,1,0:T(1,128)S(1)} %get-tuple-element.68), channel_id=1, source_target_pairs={{1,0},{2,1},{3,2},{4,3},{5,4},{6,5},{7,6},{8,7},{9,8},{10,9},{11,1... | collective-permute-start | bytes 55304 | tf_op jit(solution)/shard_map/ppermute | solution.py:26
  670.5 6.2 collective-permute-start.27
  713.8 111.4 %all-to-all-start = ((f32[8,128,2]{0,2,1:T(2,128)}), f32[8,128,2]{0,2,1:T(2,128)S(1)}, u32[]{:S(2)}, u32[]{:S(2)}) async-start(f32[8,128,2]{0,2,1:T(2,128)} %bitcast.16), calls=%async_computation | async-start | bytes 262144 | tf_op jit(solution)/shard_map/all_to_all | solution.py:164
  821.5 25.6 %collective-permute-start.29 = (f32[3,64]{0,1:T(8,128)S(1)}, f32[3,64]{0,1:T(8,128)S(1)}, u32[]{:S(2)}, u32[]{:S(2)}) collective-permute-start(f32[3,64]{0,1:T(8,128)S(1)} %slice.531), channel_id=1, source_target_pairs={{0,1},{1,2},{2,3},{3,4},{4,5},{5,6},{6,7},{7,8},{8,9},{9,10},{10,1... | collective-permute-start | bytes 2312 | tf_op jit(solution)/shard_map/ppermute | solution.py:34
  862.5 19.0 %all-to-all-start.1 = ((f32[3,128,2]{0,2,1:T(2,128)}), f32[3,128,2]{0,2,1:T(2,128)S(1)}, u32[]{:S(2)}, u32[]{:S(2)}) async-start(f32[3,128,2]{0,2,1:T(2,128)} %multiply_add_fusion.6), calls=%async_computation.1 | async-start | bytes 262144 | tf_op jit(solution)/shard_map/all_to_all | solution.py:178
  (25 other events, 559.3 us)
where the time goes:
time: 894 us; the launch traced here: 883 us
  blocking collectives  463 us (52%)
  other arithmetic  151 us (17%)
  local copies, waits for them, and re-layouts  130 us (15%)
  starting transfers between devices  102 us (11%)
  waiting for transfers between devices  26.5 us (3%)
  between operations  11.3 us (1%)
    psum x4, blocking collectives, squares(): return lax.psum(jnp.sum(residual * residual), ('grp', 'dom'))  263 us
    psum x3, blocking collectives, local(): step_size = norm_now / lax.psum(jnp.sum(direction * mapped), ('grp', 'dom'))  200 us
    scatter-add x4, other arithmetic, local(): node_force.at[:, connectivity[corner]].add(element_force[corner])  93.7 us
    gather x2, local copies, waits for them, and re-layouts, local(): corner_values = extended_disp[:, connectivity]  61.4 us
    ppermute x14, starting transfers between devices, with_halo(): lax.ppermute(lax.slice_in_dim(block, block.shape[dim] - width, None, axis...  48.9 us
    sub x1, local copies, waits for them, and re-layouts, local(): predicted - jnp.stack([0.5 * (window_at(pressure_wide, unit_step) - windo...  32.4 us
    ppermute x14, starting transfers between devices, with_halo(): lax.ppermute(lax.slice_in_dim(block, 0, width, axis=dim), axis, backward)  32.1 us
  transfers between devices with their start and end apart: 32, of which 14 were waited for; matrix products, arithmetic and copies ran while one was open for 25% of the time, Pallas kernels for 0%

commit v1 on v0

v1 whole, which is shorter than its diff:
```python
import functools

import jax
import jax.numpy as jnp
from jax import lax
from jax.experimental import pallas as pl
from jax.experimental.pallas import tpu as pltpu
from jax.sharding import PartitionSpec as P

MESH = pl.DeviceIdType.MESH
NGRP, NDOM = 4, 32
NDEV = NGRP * NDOM
CX, CY, HZ = 16, 32, 128
PX, PY, OX, OY = CX + 4, CY + 16, 2, 8
SLOT = {0: 0, 2: 1, 1: 2}
SHIFT, HALF = 6.26, 6.24
DELAY = 0.1
PAIRS = [(i, j) for i in range(4) for j in range(i, 5)]


def rows_of(ref):
    return ref.reshape(PX * 2 * PY, HZ)


class Plane:
    def __init__(self, x, y, n):
        self.x, self.y, self.n = x, y, n

    def get(self, f, dx=0, dy=0):
        return [f[self.x + dx, h, self.y + dy:self.y + dy + self.n, :] for h in (0, 1)]

    def put(self, f, halves):
        for h in (0, 1):
            f[self.x, h, self.y:self.y + self.n, :] = halves[h]


class Strip:
    def __init__(self, y):
        self.y = y

    def at(self, dx, dy, h):
        return pl.ds(((OX + dx) * 2 + h) * PY + self.y + dy, CX, stride=2 * PY)

    def get(self, f, dx=0, dy=0):
        flat = rows_of(f)
        return [flat[self.at(dx, dy, h), :] for h in (0, 1)]

    def put(self, f, halves):
        flat = rows_of(f)
        for h in (0, 1):
            flat[self.at(0, 0, h), :] = halves[h]


def lanes(a):
    return lax.broadcasted_iota(jnp.int32, a.shape, 1)


def up(a):
    r0, r1 = (pltpu.roll(v, HZ - 1, 1) for v in a)
    edge = lanes(a[0]) == HZ - 1
    return [jnp.where(edge, r1, r0), jnp.where(edge, 0.0, r1)]


def down(a):
    r0, r1 = (pltpu.roll(v, 1, 1) for v in a)
    edge = lanes(a[0]) == 0
    return [jnp.where(edge, 0.0, r0), jnp.where(edge, r0, r1)]


def each(fn, *lists):
    return [fn(*vals) for vals in zip(*lists)]


def pairs_of(region, f):
    centre = region.get(f)
    return centre, (
        (region.get(f, 1, 0), region.get(f, -1, 0)),
        (region.get(f, 0, 1), region.get(f, 0, -1)),
        (up(centre), down(centre)),
    )


def predict(region, vel, c, out):
    others = [region.get(vel.at[SLOT[d]]) for d in range(3)]
    centre, sides = pairs_of(region, vel.at[SLOT[c]])
    res = []
    for h in (0, 1):
        lap = -6.0 * centre[h]
        adv = None
        for d in range(3):
            a, b = sides[d][0][h], sides[d][1][h]
            lap = lap + a + b
            term = others[d][h] * (0.5 * (a - b))
            adv = term if adv is None else adv + term
        res.append(centre[h] + DELAY * (lap - adv))
    region.put(out.at[SLOT[c]], res)


def apply(region, damp, f):
    centre, sides = pairs_of(region, f)
    dv = region.get(damp)
    res = []
    for h in (0, 1):
        s = None
        for a, b in sides:
            s = a[h] + b[h] if s is None else s + a[h] + b[h]
        res.append(((dv[h] + (6.0 - SHIFT)) * centre[h] - s) * (1.0 / HALF))
    return res


def cheb(region, damp, f, before, out):
    res = apply(region, damp, f)
    if before is not None:
        res = each(lambda a, b: 2.0 * a - b, res, region.get(before))
    if out is not None:
        region.put(out, res)
    return res


def all_planes(fn, lo=OX, hi=OX + CX, parts=2):
    def body(x, carry):
        for k in range(parts):
            fn(Plane(x, OY + k * (CY // parts), CY // parts))
        return carry

    lax.fori_loop(lo, hi, body, 0)


def position():
    return lax.axis_index("grp"), lax.axis_index("dom")


def clear_outside(f):
    g, d = position()

    @pl.when(g == 0)
    def _():
        f[0:OX] = jnp.zeros((OX, 2, PY, HZ), jnp.float32)

    @pl.when(g == NGRP - 1)
    def _():
        f[OX + CX:PX] = jnp.zeros((PX - OX - CX, 2, PY, HZ), jnp.float32)

    @pl.when(d == 0)
    def _():
        f[:, :, 0:OY, :] = jnp.zeros((PX, 2, OY, HZ), jnp.float32)

    @pl.when(d == NDOM - 1)
    def _():
        f[:, :, OY + CY:PY, :] = jnp.zeros((PX, 2, PY - OY - CY, HZ), jnp.float32)


def neighbour(dg, dd):
    g, d = position()
    return lax.rem(g + dg + NGRP, NGRP), lax.rem(d + dd + NDOM, NDOM)


def sides_of(ref, lead, width):
    lo, hi = OX, OX + CX
    a, b = OY, OY + CY
    ys = slice(a, b)
    xs = slice(lo, hi)
    w = width
    return [
        ((1, 0), lead + (slice(hi - w, hi), slice(None), ys), lead + (slice(lo - w, lo), slice(None), ys)),
        ((-1, 0), lead + (slice(lo, lo + w), slice(None), ys), lead + (slice(hi, hi + w), slice(None), ys)),
        ((0, 1), lead + (xs, slice(None), slice(b - w, b)), lead + (xs, slice(None), slice(a - w, a))),
        ((0, -1), lead + (xs, slice(None), slice(a, a + w)), lead + (xs, slice(None), slice(b, b + w))),
    ]


def corners_of(ref, lead):
    out = []
    for dg in (1, -1):
        for dd in (1, -1):
            sx = OX + CX - 1 if dg == 1 else OX
            tx = OX - 1 if dg == 1 else OX + CX
            sy = OY + CY - 1 if dd == 1 else OY
            ty = OY - 1 if dd == 1 else OY + CY
            out.append((
                (dg, dd),
                lead + (slice(sx, sx + 1), slice(None), slice(sy, sy + 1)),
                lead + (slice(tx, tx + 1), slice(None), slice(ty, ty + 1)),
            ))
    return out


def start_all(ref, items, send, recv, base):
    copies = []
    for k, (way, src, dst) in enumerate(items):
        cp = pltpu.make_async_remote_copy(
            src_ref=ref.at[src], dst_ref=ref.at[dst],
            send_sem=send.at[base + k], recv_sem=recv.at[base + k],
            device_id=neighbour(*way), device_id_type=MESH,
        )
        cp.start()
        copies.append(cp)
    return copies


def greet_all():
    g, d = position()
    me = g * NDOM + d
    barrier = pltpu.get_barrier_semaphore()

    def body(i, carry):
        t = lax.rem(me + i, NDEV)
        pl.semaphore_signal(barrier, inc=1, device_id=(t // NDOM, lax.rem(t, NDOM)), device_id_type=MESH)
        return carry

    lax.fori_loop(1, NDEV, body, 0, unroll=8)
    return barrier


def exchange_start(out_ref, in_ref, own, send, recv):
    g, d = position()
    me = g * NDOM + d
    mine = pltpu.make_async_copy(out_ref.at[pl.ds(me, 1)], in_ref.at[pl.ds(me, 1)], own)
    mine.start()

    def body(i, carry):
        t = lax.rem(me + i, NDEV)
        pltpu.make_async_remote_copy(
            src_ref=out_ref.at[pl.ds(t, 1)], dst_ref=in_ref.at[pl.ds(me, 1)],
            send_sem=send, recv_sem=recv,
            device_id=(t // NDOM, lax.rem(t, NDOM)), device_id_type=MESH,
        ).start()
        return carry

    lax.fori_loop(1, NDEV, body, 0, unroll=8)
    return mine


def exchange_wait(mine, out_ref, in_ref, send, recv):
    rest = pl.ds(0, NDEV - 1)
    mine.wait()
    pltpu.make_async_copy(out_ref.at[rest], in_ref.at[rest], recv).wait()
    pltpu.make_async_copy(out_ref.at[rest], in_ref.at[rest], send).wait()


def iterate(gram):
    def times(v):
        out = [None] * 5

        def put(i, val):
            out[i] = val if out[i] is None else out[i] + val

        for j, val in enumerate(v):
            if val is None:
                continue
            put(j, SHIFT * val)
            if j == 0:
                put(1, HALF * val)
            else:
                put(j + 1, (0.5 * HALF) * val)
                put(j - 1, (0.5 * HALF) * val)
        return out

    worst = None

    def form(a, b):
        nonlocal worst
        total = size = None
        for i in range(5):
            for j in range(5):
                if a[i] is None or b[j] is None:
                    continue
                term = a[i] * b[j] * gram(min(i, j), max(i, j))
                total = term if total is None else total + term
                mag = jnp.abs(term)
                size = mag if size is None else size + mag
        ratio = total / size
        worst = ratio if worst is None else jnp.minimum(worst, ratio)
        return total

    def axpy(a, s, b):
        return [x if y is None else (s * y if x is None else x + s * y) for x, y in zip(a, b)]

    one = jnp.ones_like(gram(0, 0))
    r = [one, None, None, None, None]
    d = list(r)
    p = [None] * 5
    rr = gram(0, 0)
    for k in range(4):
        m = times(d)
        step = rr / form(d, m)
        p = axpy(p, step, d)
        if k == 3:
            break
        r = axpy(r, -step, m)
        new = form(r, r)
        d = axpy(r, new / rr, d)
        rr = new
    return p[:4], worst


def fluid_kernel(vel_hbm, damp_hbm, nv_hbm, p_hbm, flag_ref, vel, damp, pred, basis, press, nvel,
                 rows_out, rows_in, lsem, ssem, rsem, asem):
    barrier = greet_all()
    loads = []
    for h in (0, 1):
        z = slice(h * HZ, (h + 1) * HZ)
        for c in range(3):
            loads.append(pltpu.make_async_copy(
                vel_hbm.at[c, :, :, z], vel.at[SLOT[c], OX:OX + CX, h, OY:OY + CY, :], lsem.at[len(loads)]))
        loads.append(pltpu.make_async_copy(
            damp_hbm.at[:, :, z], damp.at[OX:OX + CX, h, OY:OY + CY, :], lsem.at[len(loads)]))
    for cp in loads:
        cp.start()
    for cp in loads:
        cp.wait()
    pl.semaphore_wait(barrier, NDEV - 1)

    one = slice(None)
    f_x, f_y, f_z = SLOT[0], SLOT[1], SLOT[2]
    faces = corners_of(vel, (one,))
    wide_x, wide_y = sides_of(vel, (f_x,), 2)[:2], sides_of(vel, (f_y,), 2)[2:]
    thin_x, thin_y = sides_of(vel, (slice(1, 3),), 1)[:2], sides_of(vel, (slice(0, 2),), 1)[2:]
    copies = start_all(vel, faces + wide_x + wide_y + thin_x + thin_y, ssem, rsem, 0)
    copies += start_all(damp, sides_of(damp, (), 1), ssem, rsem, 12)
    for cp in copies:
        cp.wait()
    for c in range(3):
        clear_outside(vel.at[c])

    def pred_main(region):
        for c in range(3):
            predict(region, vel, c, pred)

    all_planes(pred_main)
    for x in (OX - 1, OX + CX):
        for k in range(2):
            predict(Plane(x, OY + 16 * k, 16), vel, 0, pred)
    for y in (OY - 1, OY + CY):
        predict(Strip(y), vel, 1, pred)
    clear_outside(pred.at[f_x])
    clear_outside(pred.at[f_y])

    t0, t1, t2, t3 = (basis.at[j] for j in range(4))

    def diverge(region):
        fx, fy, fz = pred.at[f_x], pred.at[f_y], region.get(pred.at[f_z])
        s = each(lambda a, b: 0.5 * (a - b), region.get(fx, 1, 0), region.get(fx, -1, 0))
        s = each(lambda s, a, b: s + 0.5 * (a - b), s, region.get(fy, 0, 1), region.get(fy, 0, -1))
        s = each(lambda s, a, b: -(s + 0.5 * (a - b)), s, up(fz), down(fz))
        region.put(t0, s)

    all_planes(diverge)

    def swap(f, base):
        cps = start_all(f, corners_of(f, ()) + sides_of(f, (), 2), ssem, rsem, base)
        for cp in cps:
            cp.wait()
        clear_outside(f)

    def grow(f, before, out):
        all_planes(lambda region: cheb(region, damp, f, before, out), OX - 1, OX + CX + 1)
        for y in (OY - 1, OY + CY):
            cheb(Strip(y), damp, f, before, out)
        clear_outside(out)

    swap(t0, 16)
    grow(t0, None, t1)
    all_planes(lambda region: cheb(region, damp, t1, t0, t2))
    swap(t2, 24)
    grow(t2, t1, t3)

    def dots(x, acc):
        acc = list(acc)
        for k in range(2):
            region = Plane(x, OY + 16 * k, 16)
            ts = [region.get(t) for t in (t0, t1, t2, t3)]
            ts.append(cheb(region, damp, t3, t2, None))
            for n, (i, j) in enumerate(PAIRS):
                for h in (0, 1):
                    prod = ts[i][h] * ts[j][h]
                    acc[n] = acc[n] + (prod[0:8] + prod[8:16])
        return tuple(acc)

    acc = lax.fori_loop(OX, OX + CX, dots, tuple(jnp.zeros((8, HZ), jnp.float32) for _ in PAIRS))
    lane = lax.broadcasted_iota(jnp.int32, (1, HZ), 1)
    row = jnp.zeros((1, HZ), jnp.float32)
    for n in range(len(PAIRS)):
        row = row + jnp.where(lane == n, jnp.sum(jnp.sum(acc[n], axis=0, keepdims=True), axis=1, keepdims=True), 0.0)
    rows_out[...] = jnp.broadcast_to(row, (NDEV, HZ))
    mine = exchange_start(rows_out, rows_in, lsem.at[8], asem.at[0], asem.at[1])
    exchange_wait(mine, rows_out, rows_in, asem.at[0], asem.at[1])
    total = jnp.sum(rows_in[...], axis=0, keepdims=True)
    gram = {}
    for n, key in enumerate(PAIRS):
        gram[key] = jnp.broadcast_to(jnp.sum(jnp.where(lane == n, total, 0.0), axis=1, keepdims=True), (1, HZ))
    coef, worst = iterate(lambda i, j: gram[(i, j)])
    flag_ref[...] = jnp.broadcast_to(worst, (8, HZ))

    def combine(region):
        res = None
        for c, t in zip(coef, (t0, t1, t2, t3)):
            vals = [c * v for v in region.get(t)]
            res = vals if res is None else each(lambda a, b: a + b, res, vals)
        region.put(press, res)

    all_planes(combine, OX - 1, OX + CX + 1)
    for y in (OY - 1, OY + CY):
        combine(Strip(y))

    def correct(region):
        _, sides = pairs_of(region, press)
        for c in range(3):
            own = region.get(pred.at[SLOT[c]])
            new = each(lambda v, a, b: v - 0.5 * (a - b), own, sides[c][0], sides[c][1])
            for h in (0, 1):
                nvel[c, region.x - OX, h, region.y - OY:region.y - OY + region.n, :] = new[h]

    all_planes(correct)
    stores = []
    for h in (0, 1):
        z = slice(h * HZ, (h + 1) * HZ)
        stores.append(pltpu.make_async_copy(nvel.at[:, :, h], nv_hbm.at[:, :, :, z], lsem.at[2 * h]))
        stores.append(pltpu.make_async_copy(
            press.at[OX:OX + CX, h, OY:OY + CY, :], p_hbm.at[:, :, z], lsem.at[2 * h + 1]))
    for cp in stores:
        cp.start()
    for cp in stores:
        cp.wait()


def fluid(velocity, damping):
    field = (PX, 2, PY, HZ)
    f32 = jnp.float32
    anywhere = pl.BlockSpec(memory_space=pl.ANY)
    return pl.pallas_call(
        fluid_kernel,
        out_shape=(
            jax.ShapeDtypeStruct(velocity.shape, f32),
            jax.ShapeDtypeStruct(damping.shape, f32),
            jax.ShapeDtypeStruct((8, HZ), f32),
        ),
        in_specs=[anywhere] * 2,
        out_specs=(anywhere, anywhere, pl.BlockSpec(memory_space=pltpu.VMEM)),
        scratch_shapes=[
            pltpu.VMEM((3,) + field, f32),
            pltpu.VMEM(field, f32),
            pltpu.VMEM((3,) + field, f32),
            pltpu.VMEM((4,) + field, f32),
            pltpu.VMEM(field, f32),
            pltpu.VMEM((3, CX, 2, CY, HZ), f32),
            pltpu.VMEM((NDEV, HZ), f32),
            pltpu.VMEM((NDEV, HZ), f32),
            pltpu.SemaphoreType.DMA((9,)),
            pltpu.SemaphoreType.DMA((32,)),
            pltpu.SemaphoreType.DMA((32,)),
            pltpu.SemaphoreType.DMA((2,)),
        ],
        compiler_params=pltpu.CompilerParams(
            collective_id=0, has_side_effects=True, vmem_limit_bytes=48 << 20),
        name="fluid",
    )(velocity, damping)


RIM = 64
RBFW = 4
WALL_FRICTION = 0.5
SHELL_STEP = 0.5


def from_behind(value, axis, steps):
    count = lax.axis_size(axis)
    leading, last = (max(0, -steps), min(count, count - steps))
    return lax.ppermute(value, axis, [(source, source + steps) for source in range(leading, last)])


def local(
    velocity,
    damping,
    displacement,
    stiffness,
    connectivity,
    inv_mass,
    iface_cell,
    iface_owner,
    iface_node,
    rbf_weight,
    normals,
):
    shell_nodes = displacement.shape[1]
    rim_values = from_behind(displacement[:, :RIM], ("grp", "dom"), -1)
    extended_disp = jnp.concatenate([displacement, rim_values], axis=1)
    element_count = connectivity.shape[1]
    corner_values = extended_disp[:, connectivity]
    element_dofs = jnp.transpose(corner_values, (1, 0, 2)).reshape(12, element_count)
    element_force = jnp.sum(stiffness * element_dofs[None], axis=1).reshape(4, 3, element_count)
    node_force = jnp.zeros((3, shell_nodes + RIM), jnp.float32)
    for corner in range(4):
        node_force = node_force.at[:, connectivity[corner]].add(element_force[corner])
    rim_force = from_behind(node_force[:, shell_nodes:], ("grp", "dom"), 1)
    stiff_force = node_force[:, :shell_nodes] + jnp.pad(rim_force, ((0, 0), (0, shell_nodes - RIM)))
    new_velocity, pressure, _ = fluid(velocity, damping)
    pressure_at = pressure.reshape(-1)[iface_cell]
    velocity_at = new_velocity.reshape(3, -1)[:, iface_cell]
    traction = -pressure_at[None] * normals + WALL_FRICTION * velocity_at
    owner_dev = iface_owner[:, 0]
    point_count = owner_dev.shape[0]
    devices = lax.axis_size("grp") * lax.axis_size("dom")
    owner_cap = max(2, 2 * point_count // devices)
    order_index = lax.iota(jnp.int32, point_count)
    earlier = (owner_dev[None, :] == owner_dev[:, None]) & (
        order_index[None, :] < order_index[:, None]
    )
    slot_rank = jnp.sum(earlier.astype(jnp.int32), axis=1)
    slot_index = owner_dev * owner_cap + slot_rank
    slot_count = devices * owner_cap
    payload = jnp.concatenate([traction, rbf_weight, iface_node.astype(jnp.float32)[None]], axis=0)
    outgoing = jnp.zeros((payload.shape[0], slot_count), jnp.float32).at[:, slot_index].set(payload)
    received = lax.all_to_all(outgoing, ("grp", "dom"), split_axis=1, concat_axis=1, tiled=True)
    slot_traction = received[:3]
    slot_weight = received[3 : 3 + RBFW]
    slot_node = received[3 + RBFW].astype(jnp.int32)
    applied = jnp.zeros((3, shell_nodes), jnp.float32)
    for offset in range(RBFW):
        applied = applied.at[:, slot_node + offset].add(slot_weight[offset][None] * slot_traction)
    node_velocity = inv_mass[None] * (applied - stiff_force)
    new_displacement = displacement + SHELL_STEP * node_velocity
    slot_velocity = jnp.zeros((3, slot_count), jnp.float32)
    for offset in range(RBFW):
        slot_velocity = (
            slot_velocity + slot_weight[offset][None] * node_velocity[:, slot_node + offset]
        )
    returned_vals = lax.all_to_all(
        slot_velocity, ("grp", "dom"), split_axis=1, concat_axis=1, tiled=True
    )
    iface_velocity = returned_vals[:, slot_index]
    return (new_velocity, pressure, new_displacement, iface_velocity)


def solution(mesh):
    return jax.shard_map(
        local,
        mesh=mesh,
        in_specs=(
            P(None, "grp", "dom", None),
            P("grp", "dom", None),
            P(None, ("grp", "dom")),
            P(None, None, ("grp", "dom")),
            P(None, ("grp", "dom")),
            P(("grp", "dom")),
            P(("grp", "dom")),
            P(("grp", "dom"), None),
            P(("grp", "dom")),
            P(None, ("grp", "dom")),
            P(None, ("grp", "dom")),
        ),
        out_specs=(
            P(None, "grp", "dom", None),
            P("grp", "dom", None),
            P(None, ("grp", "dom")),
            P(None, ("grp", "dom")),
        ),
        check_vma=False,
    )
```

time: 894 us -> 335 us (0.37); the launches traced: 883 us -> 334 us
  blocking collectives: 463 us -> 0 us
  starting transfers between devices: 102 us -> 27.3 us
  Pallas kernels: 0 us -> 44.2 us
  other arithmetic: 151 us -> 122 us
  waiting for transfers between devices: 26.5 us -> 7.1 us
  between operations: 11.3 us -> 1.09 us
    psum x7 -> x0, blocking collectives: 463 us -> none  [the longest x4 263 us: squares(): return lax.psum(jnp.sum(residual * residual), ('grp', 'dom'))]
    ppermute x28 -> x0, starting transfers between devices: 81 us -> none  [the longest x14 48.9 us: with_halo(): lax.ppermute(lax.slice_in_dim(block, block.shape[dim] - width, None, axis...]
    pallas_call x0 -> x1, Pallas kernels: none -> 44.2 us  [fluid(): pl.pallas_call(fluid_kernel, out_shape=(jax.ShapeDtypeStruct(velocity.sha...]
    reshape x0 -> x1, local copies, waits for them, and re-layouts: none -> 32.4 us  [local(): velocity_at = new_velocity.reshape(3, -1)[:, iface_cell]]
    sub x1 -> x0, local copies, waits for them, and re-layouts: 32.4 us -> none  [local(): predicted - jnp.stack([0.5 * (window_at(pressure_wide, unit_step) - windo...]
    ppermute x28 -> x0, waiting for transfers between devices: 17.9 us -> none  [the longest x14 9.69 us: with_halo(): lax.ppermute(lax.slice_in_dim(block, 0, width, axis=dim), axis, backward)]
    reduce_sum x7 -> x0, other arithmetic: 13 us -> none  [the longest x4 6.57 us: local(): step_size = norm_now / lax.psum(jnp.sum(direction * mapped), ('grp', 'dom'))]
  transfers between devices with their start and end apart: 32 -> 4, of which waited for: 14 -> 2; matrix products, arithmetic and copies ran while one was open for 25% -> 59% of each run, Pallas kernels for 0% -> 0%
where the time goes in v1:
time: 335 us; the launch traced here: 334 us
  local copies, waits for them, and re-layouts  132 us (39%)
  other arithmetic  122 us (36%)
  Pallas kernels  44.2 us (13%)
  starting transfers between devices  27.3 us (8%)
  waiting for transfers between devices  7.1 us (2%)
    scatter-add x4, other arithmetic, local(): node_force.at[:, connectivity[corner]].add(element_force[corner])  94.1 us
    gather x2, local copies, waits for them, and re-layouts, local(): corner_values = extended_disp[:, connectivity]  61.3 us
    pallas_call x1, Pallas kernels, fluid(): pl.pallas_call(fluid_kernel, out_shape=(jax.ShapeDtypeStruct(velocity.sha...  44.2 us
    reshape x1, local copies, waits for them, and re-layouts, local(): velocity_at = new_velocity.reshape(3, -1)[:, iface_cell]  32.4 us
    scatter-add x4, other arithmetic, local(): applied.at[:, slot_node + offset]  17.1 us
    all_to_all x1, starting transfers between devices, local(): lax.all_to_all(slot_velocity, ('grp', 'dom'), split_axis=1, concat_axis=1...  13.4 us
    unnamed x28, local copies, waits for them, and re-layouts  10.2 us
    gather x4, local copies, waits for them, and re-layouts, local(): node_velocity[:, slot_node + offset]  9.24 us
  transfers between devices with their start and end apart: 4, of which 2 were waited for; matrix products, arithmetic and copies ran while one was open for 59% of the time, Pallas kernels for 0%

profile of v1, /device:TPU:1, one launch (start us, length us, event | category | flops | bytes accessed | tf_op | source)
XLA Modules:
  0.0 334.4 jit_solution(8887933825639211335)
XLA Ops:
  3.1 44.2 %fluid.1 = (f32[3,16,32,256]{3,2,1,0:T(8,128)S(1)}, f32[16,32,256]{2,1,0:T(8,128)S(1)}, f32[8,128]{1,0:T(8,128)}) custom-call(f32[3,16,32,256]{3,2,1,0:T(8,128)S(1)} %copy-done, f32[16,32,256]{2,1,0:T(8,128)S(1)} %copy-done.1), custom_call_target="tpu_custom_call" | custom-call | tf_op jit(solution)/shard_map/fluid/pallas_call | solution.py:431
  47.3 32.4 %copy.179 = f32[3,16,32,256]{0,3,2,1:T(8,128)} copy(f32[3,16,32,256]{3,2,1,0:T(8,128)S(1)} %get-tuple-element.66) | data formatting | bytes 3145728 | tf_op jit(solution)/shard_map/reshape | solution.py:499
  84.9 8.4 %all-to-all-start = ((f32[8,128,2]{0,2,1:T(2,128)}), f32[8,128,2]{0,2,1:T(2,128)S(1)}, u32[]{:S(2)}, u32[]{:S(2)}) async-start(f32[8,128,2]{0,2,1:T(2,128)} %bitcast.7), calls=%async_computation | async-start | bytes 262144 | tf_op jit(solution)/shard_map/all_to_all | solution.py:514
  93.3 3.0 collective-permute-start
  100.6 56.0 %gather_fusion.2 = f32[16384,3]{1,0:T(8,128)} fusion(f32[3,4160]{0,1:T(8,128)} %copy.162, s32[16384]{0:T(1024)S(1)} %broadcast_clamp_fusion), kind=kCustom, calls=%fused_computation.2 | custom fusion | bytes 458752 | tf_op jit(solution)/shard_map/gather | solution.py:489
  156.6 5.3 %copy.163 = f32[4,4096,3]{1,2,0:T(4,128)S(1)} copy(f32[4,4096,3]{2,1,0:T(8,128)} %bitcast.75) | data formatting | bytes 393216 | tf_op jit(solution)/shard_map/gather | solution.py:489
  162.0 2.6 multiply_reduce_fusion
  172.6 24.1 %scatter_custom_fusion.5 = f32[3,4160]{0,1:T(8,128)} fusion(s32[4096]{0:T(1024)S(1)} %bitcast.89, f32[4096,3]{1,0:T(8,128)} %copy.164, f32[]{:T(128)} %constant.13.clone.1), kind=kCustom, calls=%fused_computation.22 | custom fusion | flops 12288 | bytes 50432 | tf_op jit(solution)/shard_map/scatter-add | solution.py:494
  196.7 23.3 %scatter_fusion.3 = f32[3,4160]{0,1:T(8,128)} fusion(f32[3,4160]{0,1:T(8,128)} %scatter_custom_fusion.5, s32[4096]{0:T(1024)S(1)} %bitcast.88, f32[4096,3]{1,0:T(8,128)} %copy.165), kind=kCustom, calls=%fused_computation.14 | custom fusion | flops 12288 | bytes 163840 | tf_op jit(solution)/shard_map/scatter-add | solution.py:494
  220.1 23.3 %scatter_fusion.4 = f32[3,4160]{0,1:T(8,128)} fusion(f32[3,4160]{0,1:T(8,128)} %scatter_fusion.3, s32[4096]{0:T(1024)S(1)} %bitcast.87, f32[4096,3]{1,0:T(8,128)} %copy.166), kind=kCustom, calls=%fused_computation.15 | custom fusion | flops 12288 | bytes 163840 | tf_op jit(solution)/shard_map/scatter-add | solution.py:494
  243.4 23.3 %scatter_fusion.5 = f32[3,4160]{0,1:T(8,128)} fusion(f32[3,4160]{0,1:T(8,128)} %scatter_fusion.4, s32[4096]{0:T(1024)S(1)} %bitcast.86, f32[4096,3]{1,0:T(8,128)} %copy.167), kind=kCustom, calls=%fused_computation.16 | custom fusion | flops 12288 | bytes 163840 | tf_op jit(solution)/shard_map/scatter-add | solution.py:494
  267.5 2.5 collective-permute-start.1
  271.9 2.4 fusion.6
  274.6 3.0 scatter_custom_fusion.1
  278.1 4.7 %scatter_fusion = f32[3,4096]{0,1:T(8,128)} fusion(f32[3,4096]{0,1:T(8,128)} %scatter_custom_fusion.1, s32[256]{0:T(256)S(1)} %bitcast.95, f32[256,3]{1,0:T(8,128)S(1)} %copy.159), kind=kCustom, calls=%fused_computation.10 | custom fusion | flops 768 | bytes 10240 | tf_op jit(solution)/shard_map/scatter-add | solution.py:520
  282.8 4.7 %scatter_fusion.1 = f32[3,4096]{0,1:T(8,128)} fusion(f32[3,4096]{0,1:T(8,128)} %scatter_fusion, s32[256]{0:T(256)S(1)} %bitcast.93, f32[256,3]{1,0:T(8,128)S(1)} %copy.160), kind=kCustom, calls=%fused_computation.11 | custom fusion | flops 768 | bytes 10240 | tf_op jit(solution)/shard_map/scatter-add | solution.py:520
  287.5 4.7 %scatter_fusion.2 = f32[3,4096]{0,1:T(8,128)} fusion(f32[3,4096]{0,1:T(8,128)} %scatter_fusion.1, s32[256]{0:T(256)S(1)} %bitcast.91, f32[256,3]{1,0:T(8,128)S(1)} %copy.161), kind=kCustom, calls=%fused_computation.12 | custom fusion | flops 768 | bytes 10240 | tf_op jit(solution)/shard_map/scatter-add | solution.py:520
  292.2 4.4 %multiply_add_fusion = (f32[3,4096]{0,1:T(8,128)}, f32[3,4096]{0,1:T(8,128)}) fusion(f32[3,4096]{0,1:T(8,128)} %copy.168, f32[3,4096]{0,1:T(8,128)} %scatter_fusion.2, f32[3,64]{0,1:T(8,128)S(1)} %collective-permute-done.1, f32[3,4160]{0,1:T(8,128)} %scatter_fusion.5, f32[4096]{0:T(1024)S(1)} %copy-done.4), kind=kLoop, calls=%fused_computation.21 | loop fusion | flops 61440 | bytes 262912 | tf_op jit(solution)/shard_map/add | solution.py:522
  298.9 2.3 gather_fusion.4
  301.2 2.3 gather_fusion.5
  303.5 2.3 gather_fusion.6
  307.9 13.4 %all-to-all-start.1 = ((f32[3,128,2]{0,2,1:T(2,128)}), f32[3,128,2]{0,2,1:T(2,128)S(1)}, u32[]{:S(2)}, u32[]{:S(2)}) async-start(f32[3,128,2]{0,2,1:T(2,128)} %multiply_add_fusion.1), calls=%async_computation.1 | async-start | bytes 262144 | tf_op jit(solution)/shard_map/all_to_all | solution.py:528
  321.4 2.8 copy.177
  324.2 7.0 %all-to-all-done.1 = f32[3,128,2]{0,2,1:T(2,128)S(1)} async-done(((f32[3,128,2]{0,2,1:T(2,128)}), f32[3,128,2]{0,2,1:T(2,128)S(1)}, u32[]{:S(2)}, u32[]{:S(2)}) %all-to-all-start.1) | async-done | bytes 3104 | tf_op jit(solution)/shard_map/all_to_all | solution.py:528
  (85 shorter events, 30.8 us)
Async XLA Ops:
  0.6 1.4 copy-start
  2.0 1.0 copy-start.1
  47.3 32.4 %copy-start.7 = (s32[128]{0:T(128)S(1)}, s32[128]{0:T(128)}, u32[]{:S(2)}) copy-start(s32[128]{0:T(128)} %param.17) | copy-start | bytes 1540
  47.3 35.7 %copy-start.8 = (s32[128]{0:T(128)S(1)}, s32[128]{0:T(128)}, u32[]{:S(2)}) copy-start(s32[128]{0:T(128)} %param.19) | copy-start | bytes 1540
  47.3 35.7 %copy-start.6 = (f32[3,128]{1,0:T(4,128)S(1)}, f32[3,128]{1,0:T(4,128)}, u32[]{:S(2)}) copy-start(f32[3,128]{1,0:T(4,128)} %param.21) | copy-start | bytes 4612
  47.3 35.7 %copy-start.5 = (f32[4,128]{1,0:T(4,128)S(1)}, f32[4,128]{1,0:T(4,128)}, u32[]{:S(2)}) copy-start(f32[4,128]{1,0:T(4,128)} %param.20) | copy-start | bytes 6148
  47.3 35.9 %copy-start.9 = (s32[128,1]{0,1:T(1,128)S(1)}, s32[128,1]{0,1:T(1,128)}, u32[]{:S(2)}) copy-start(s32[128,1]{0,1:T(1,128)} %param.18) | copy-start | bytes 1540
  79.7 13.6 %copy-start.2 = (f32[3,4096]{1,0:T(4,128)S(1)}, f32[3,4096]{1,0:T(4,128)}, u32[]{:S(2)}) copy-start(f32[3,4096]{1,0:T(4,128)} %param.13) | copy-start | bytes 147460
  79.7 16.6 %copy-start.3 = (s32[4,4096]{1,0:T(4,128)S(1)}, s32[4,4096]{1,0:T(4,128)}, u32[]{:S(2)}) copy-start(s32[4,4096]{1,0:T(4,128)} %param.15) | copy-start | bytes 196612
  84.9 185.1 %all-to-all-start = ((f32[8,128,2]{0,2,1:T(2,128)}), f32[8,128,2]{0,2,1:T(2,128)S(1)}, u32[]{:S(2)}, u32[]{:S(2)}) async-start(f32[8,128,2]{0,2,1:T(2,128)} %bitcast.7), calls=%async_computation | async-start | bytes 262144 | tf_op jit(solution)/shard_map/all_to_all | solution.py:514
  93.3 5.2 %collective-permute-start = (f32[3,64]{1,0:T(4,128)S(1)}, f32[3,64]{1,0:T(4,128)S(1)}, u32[]{:S(2)}, u32[]{:S(2)}) collective-permute-start(f32[3,64]{1,0:T(4,128)S(1)} %slice.80), channel_id=1, source_target_pairs={{1,0},{2,1},{3,2},{4,3},{5,4},{6,5},{7,6},{8,7},{9,8},{10,9},{11,1... | collective-permute-start | bytes 2312 | tf_op jit(solution)/shard_map/ppermute | solution.py:469
  267.5 24.6 %collective-permute-start.1 = (f32[3,64]{0,1:T(8,128)S(1)}, f32[3,64]{0,1:T(8,128)S(1)}, u32[]{:S(2)}, u32[]{:S(2)}) collective-permute-start(f32[3,64]{0,1:T(8,128)S(1)} %slice.117), channel_id=1, source_target_pairs={{0,1},{1,2},{2,3},{3,4},{4,5},{5,6},{6,7},{7,8},{8,9},{9,10},{10,1... | collective-permute-start | bytes 2312 | tf_op jit(solution)/shard_map/ppermute | solution.py:469
  271.2 21.0 %copy-start.4 = (f32[4096]{0:T(1024)S(1)}, f32[4096]{0:T(1024)}, u32[]{:S(2)}) copy-start(f32[4096]{0:T(1024)} %param.16) | copy-start | bytes 49156
  307.9 23.2 %all-to-all-start.1 = ((f32[3,128,2]{0,2,1:T(2,128)}), f32[3,128,2]{0,2,1:T(2,128)S(1)}, u32[]{:S(2)}, u32[]{:S(2)}) async-start(f32[3,128,2]{0,2,1:T(2,128)} %multiply_add_fusion.1), calls=%async_computation.1 | async-start | bytes 262144 | tf_op jit(solution)/shard_map/all_to_all | solution.py:528

commit v2 on v1

--- a/solution.py
+++ b/solution.py
@@ -1,5 +1,3 @@
-import functools
-
 import jax
 import jax.numpy as jnp
 from jax import lax
@@ -14,7 +12,11 @@
 PX, PY, OX, OY = CX + 4, CY + 16, 2, 8
 SLOT = {0: 0, 2: 1, 1: 2}
 SHIFT, HALF = 6.26, 6.24
-DELAY = 0.1
+TIME_STEP = 0.1
+WALL_FRICTION = 0.5
+SHELL_STEP = 0.5
+RIM, RBFW, NBLK, NPTS = 64, 4, 32, 128
+W_BASIS, W_WEIGHT, W_NODE, W_NEXT = 32, 47, 51, 32
 PAIRS = [(i, j) for i in range(4) for j in range(i, 5)]
 
 
@@ -92,7 +94,7 @@
             lap = lap + a + b
             term = others[d][h] * (0.5 * (a - b))
             adv = term if adv is None else adv + term
-        res.append(centre[h] + DELAY * (lap - adv))
+        res.append(centre[h] + TIME_STEP * (lap - adv))
     region.put(out.at[SLOT[c]], res)
 
 
@@ -294,9 +296,147 @@
     return p[:4], worst
 
 
-def fluid_kernel(vel_hbm, damp_hbm, nv_hbm, p_hbm, flag_ref, vel, damp, pred, basis, press, nvel,
-                 rows_out, rows_in, lsem, ssem, rsem, asem):
+def lane_of(shape):
+    return lax.broadcasted_iota(jnp.int32, shape, 1)
+
+
+def row_of(shape):
+    return lax.broadcasted_iota(jnp.int32, shape, 0)
+
+
+def thirds(x):
+    a = x.astype(jnp.bfloat16)
+    rest = x - a.astype(jnp.float32)
+    b = rest.astype(jnp.bfloat16)
+    return a, b, (rest - b.astype(jnp.float32)).astype(jnp.bfloat16)
+
+
+def pick(onehot, x):
+    width = x.shape[1]
+    wide = jnp.concatenate(thirds(x), axis=1)
+    out = jnp.dot(onehot, wide, preferred_element_type=jnp.float32)
+    return out[:, :width] + out[:, width:2 * width] + out[:, 2 * width:]
+
+
+def spread(src, dst, count, stride):
+    for b in range(NBLK):
+        dst[pl.ds(b, count, stride=stride), :] = src[:, b * HZ:(b + 1) * HZ]
+
+
+def shell_gather(q, disp, conn, dofs):
+    sub = row_of((8, HZ))
+    for a in range(4):
+        rel = conn[a, 8 * q:8 * q + 8, :] - HZ * (8 * q + sub)
+        near = rel < HZ
+        low = jnp.where(near, rel, rel - HZ)
+        for c in range(3):
+            here = jnp.take_along_axis(disp[c, 8 * q:8 * q + 8, :], low, axis=1, mode="promise_in_bounds")
+            there = jnp.take_along_axis(disp[c, 8 * q + 1:8 * q + 9, :], low, axis=1, mode="promise_in_bounds")
+            dofs[pl.ds(8 * q * 16 + 3 * a + c, 8, stride=16), :] = jnp.where(near, here, there)
+
+
+def shell_product(q, stiff, dofs, force):
+    sub = row_of((8, HZ))
+
+    def body(i, carry):
+        parts = []
+        for b in range(8 * q, 8 * q + 8):
+            z = slice(b * HZ, (b + 1) * HZ)
+            top = stiff[i, 0:8, z] * dofs[b * 16:b * 16 + 8, :]
+            low = stiff[i, 8:12, z] * dofs[b * 16 + 8:b * 16 + 12, :]
+            parts.append(top + jnp.concatenate([low, jnp.zeros((4, HZ), jnp.float32)], axis=0))
+        first = sub < 4
+        parts = [
+            jnp.where(first, parts[k], parts[k + 4]) + pltpu.roll(jnp.where(first, parts[k + 4], parts[k]), 4, 0)
+            for k in range(4)
+        ]
+        for bit in (2, 1):
+            keep = (sub & bit) == 0
+            parts = [
+                jnp.where(keep, parts[k] + pltpu.roll(parts[k], 8 - bit, 0),
+                          parts[k + bit] + pltpu.roll(parts[k + bit], bit, 0))
+                for k in range(bit)
+            ]
+        force[i, 8 * q:8 * q + 8, :] = parts[0]
+        return carry
+
+    lax.fori_loop(0, 12, body, 0)
+
+
+def shell_scatter(q, conn, force, own, over):
+    lane = lane_of((8, HZ))
+    element = HZ * (8 * q + row_of((8, HZ))) + lane
+    rel = [conn[a, 8 * q:8 * q + 8, :] - element for a in range(4)]
+    vals = [[force[3 * a + c, 8 * q:8 * q + 8, :] for c in range(3)] for a in range(4)]
+
+    def body(d, acc):
+        hit = [r == d for r in rel]
+        inside = lane >= d
+        out = []
+        for c in range(3):
+            s = jnp.zeros((8, HZ), jnp.float32)
+            for a in range(4):
+                s = jnp.where(hit[a], vals[a][c], s)
+            s = pltpu.roll(s, d, 1)
+            out.append(acc[2 * c] + jnp.where(inside, s, 0.0))
+            out.append(acc[2 * c + 1] + jnp.where(inside, 0.0, s))
+        return tuple(out)
+
+    acc = lax.fori_loop(0, RIM + 1, body, tuple(jnp.zeros((8, HZ), jnp.float32) for _ in range(6)), unroll=5)
+    for c in range(3):
+        own[c, 8 * q:8 * q + 8, :] = acc[2 * c]
+        over[c, 8 * q + 1:8 * q + 9, :] = acc[2 * c + 1]
+
+
+def sample(cells, f, mid0, mid1, dx, dy):
+    def body(i, carry):
+        for u in range(4):
+            k = i * 4 + u
+            cell = cells[k]
+            x = lax.div(cell, CY * 2 * HZ) + OX
+            y = lax.rem(lax.div(cell, 2 * HZ), CY) + OY
+            h = lax.rem(lax.div(cell, HZ), 2)
+            at = pl.ds(k, 1)
+            mid0[at, :] = f[x, 0, pl.ds(y, 1), :]
+            mid1[at, :] = f[x, 1, pl.ds(y, 1), :]
+            dx[at, :] = f[x + 1, h, pl.ds(y, 1), :] - f[x - 1, h, pl.ds(y, 1), :]
+            dy[at, :] = f[x, h, pl.ds(y + 1, 1), :] - f[x, h, pl.ds(y - 1, 1), :]
+        return carry
+
+    lax.fori_loop(0, NPTS // 4, body, 0)
+
+
+def sample_centre(cells, fields, outs):
+    def body(i, carry):
+        for u in range(4):
+            k = i * 4 + u
+            cell = cells[k]
+            x = lax.div(cell, CY * 2 * HZ) + OX
+            y = lax.rem(lax.div(cell, 2 * HZ), CY) + OY
+            h = lax.rem(lax.div(cell, HZ), 2)
+            for f, o in zip(fields, outs):
+                o[pl.ds(k, 1), :] = f[x, h, pl.ds(y, 1), :]
+        return carry
+
+    lax.fori_loop(0, NPTS // 4, body, 0)
+
+
+def column(row):
+    return jnp.transpose(jnp.broadcast_to(row, (HZ, HZ)))
+
+
+def total_of(x):
+    return jnp.sum(x, axis=1, keepdims=True)
+
+
+def step_kernel(vel_hbm, damp_hbm, stiff_hbm, disp_in, conn_in, mass, cells, cell_row, owner, node, weight, normal,
+                nv_hbm, p_hbm, disp_out, iface_out, flag_ref,
+                vel, damp, pred, t0, t1, t2, t3, press, nvel, stiff,
+                disp, conn, dofs, force, own, over, mid0, mid1, dx, dy, words, table, nodal,
+                rows_out, rows_in, back_out, back_in, lsem, ksem, ssem, rsem, asem):
     barrier = greet_all()
+    g, d = position()
+    me = g * NDOM + d
     loads = []
     for h in (0, 1):
         z = slice(h * HZ, (h + 1) * HZ)
@@ -305,9 +445,32 @@
                 vel_hbm.at[c, :, :, z], vel.at[SLOT[c], OX:OX + CX, h, OY:OY + CY, :], lsem.at[len(loads)]))
         loads.append(pltpu.make_async_copy(
             damp_hbm.at[:, :, z], damp.at[OX:OX + CX, h, OY:OY + CY, :], lsem.at[len(loads)]))
+    for q in range(4):
+        z = slice(q * 8 * HZ, (q + 1) * 8 * HZ)
+        loads.append(pltpu.make_async_copy(stiff_hbm.at[:, :, z], stiff.at[:, :, z], ksem.at[q]))
     for cp in loads:
         cp.start()
-    for cp in loads:
+    blocks = loads[8:]
+
+    spread(disp_in, disp.reshape(3 * 40, HZ), 3, 40)
+    spread(conn_in, conn.reshape(4 * NBLK, HZ), 4, NBLK)
+    for q in range(3):
+        shell_gather(q, disp, conn, dofs)
+        blocks[q].wait()
+        shell_product(q, stiff, dofs, force)
+
+    square = (HZ, HZ)
+    owns = owner[...] == row_of(square)
+    first = jnp.min(jnp.where(owns, lane_of(square), HZ), axis=1, keepdims=True)
+    for s in (0, 1):
+        table[:, s * HZ:(s + 1) * HZ] = jnp.where(
+            owns & ((lane_of(square) == first) == (s == 0)), 1.0, 0.0).astype(jnp.bfloat16)
+    words[...] = jnp.zeros(square, jnp.float32)
+    words[W_WEIGHT:W_WEIGHT + 4, :] = weight[...]
+    words[W_NODE:W_NODE + 1, :] = node[...].astype(jnp.float32)
+    words[...] = jnp.transpose(words[...])
+
+    for cp in loads[:8]:
         cp.wait()
     pl.semaphore_wait(barrier, NDEV - 1)
 
@@ -318,6 +481,13 @@
     thin_x, thin_y = sides_of(vel, (slice(1, 3),), 1)[:2], sides_of(vel, (slice(0, 2),), 1)[2:]
     copies = start_all(vel, faces + wide_x + wide_y + thin_x + thin_y, ssem, rsem, 0)
     copies += start_all(damp, sides_of(damp, (), 1), ssem, rsem, 12)
+    before, after = lax.rem(me + NDEV - 1, NDEV), lax.rem(me + 1, NDEV)
+    rim = pltpu.make_async_remote_copy(
+        src_ref=disp.at[:, 0:1, :], dst_ref=disp.at[:, NBLK:NBLK + 1, :], send_sem=ssem.at[32], recv_sem=rsem.at[32],
+        device_id=(lax.div(before, NDOM), lax.rem(before, NDOM)), device_id_type=MESH)
+    rim.start()
+    for q in range(3):
+        shell_scatter(q, conn, force, own, over)
     for cp in copies:
         cp.wait()
     for c in range(3):
@@ -336,8 +506,6 @@
     clear_outside(pred.at[f_x])
     clear_outside(pred.at[f_y])
 
-    t0, t1, t2, t3 = (basis.at[j] for j in range(4))
-
     def diverge(region):
         fx, fy, fz = pred.at[f_x], pred.at[f_y], region.get(pred.at[f_z])
         s = each(lambda a, b: 0.5 * (a - b), region.get(fx, 1, 0), region.get(fx, -1, 0))
@@ -348,10 +516,7 @@
     all_planes(diverge)
 
     def swap(f, base):
-        cps = start_all(f, corners_of(f, ()) + sides_of(f, (), 2), ssem, rsem, base)
-        for cp in cps:
-            cp.wait()
-        clear_outside(f)
+        return start_all(f, corners_of(f, ()) + sides_of(f, (), 2), ssem, rsem, base)
 
     def grow(f, before, out):
         all_planes(lambda region: cheb(region, damp, f, before, out), OX - 1, OX + CX + 1)
@@ -359,10 +524,56 @@
             cheb(Strip(y), damp, f, before, out)
         clear_outside(out)
 
-    swap(t0, 16)
+    moving = swap(t0, 16)
+    rim.wait()
+
+    @pl.when(me == NDEV - 1)
+    def _():
+        disp[:, NBLK:NBLK + 1, :] = jnp.zeros((3, 1, HZ), jnp.float32)
+
+    shell_gather(3, disp, conn, dofs)
+    blocks[3].wait()
+    shell_product(3, stiff, dofs, force)
+    shell_scatter(3, conn, force, own, over)
+    edge = pltpu.make_async_remote_copy(
+        src_ref=over.at[:, NBLK:NBLK + 1, :], dst_ref=over.at[:, 0:1, :], send_sem=ssem.at[33], recv_sem=rsem.at[33],
+        device_id=(lax.div(after, NDOM), lax.rem(after, NDOM)), device_id_type=MESH)
+    edge.start()
+    for cp in moving:
+        cp.wait()
+    clear_outside(t0)
     grow(t0, None, t1)
     all_planes(lambda region: cheb(region, damp, t1, t0, t2))
-    swap(t2, 24)
+
+    moving = swap(t2, 24)
+    z_all = column(cell_row[...]) & (2 * HZ - 1)
+    lane = lane_of(square)
+    hit0, hit1 = lane == z_all, lane + HZ == z_all
+    hit = hit0 | hit1
+    normals = [column(normal[c:c + 1, :]) for c in range(3)]
+
+    def place(word, values):
+        words[...] += jnp.where(lane == word, total_of(values), 0.0)
+
+    def basis_words(j, f):
+        sample(cells, f, mid0, mid1, dx, dy)
+        a, b = mid0[...], mid1[...]
+        value = jnp.where(hit0, a, 0.0) + jnp.where(hit1, b, 0.0)
+        slope = (jnp.where(lane == z_all + 1, a, 0.0) + jnp.where(lane + HZ == z_all + 1, b, 0.0)
+                 - jnp.where(lane == z_all - 1, a, 0.0) - jnp.where(lane + HZ == z_all - 1, b, 0.0))
+        slopes = (jnp.where(hit, dx[...], 0.0), jnp.where(hit, dy[...], 0.0), slope)
+        for c in range(3):
+            place(W_BASIS + 3 * (j + 1) + c, -value * normals[c] - (0.5 * WALL_FRICTION) * slopes[c])
+
+    sample_centre(cells, [pred.at[SLOT[c]] for c in range(3)], [mid0, mid1, dx])
+    for c, ref in enumerate((mid0, mid1, dx)):
+        place(W_BASIS + c, jnp.where(hit, WALL_FRICTION * ref[...], 0.0))
+    basis_words(0, t0)
+    basis_words(1, t1)
+    for cp in moving:
+        cp.wait()
+    clear_outside(t2)
+    basis_words(2, t2)
     grow(t2, t1, t3)
 
     def dots(x, acc):
@@ -378,19 +589,77 @@
         return tuple(acc)
 
     acc = lax.fori_loop(OX, OX + CX, dots, tuple(jnp.zeros((8, HZ), jnp.float32) for _ in PAIRS))
-    lane = lax.broadcasted_iota(jnp.int32, (1, HZ), 1)
+    basis_words(3, t3)
+    lane1 = lane_of((1, HZ))
     row = jnp.zeros((1, HZ), jnp.float32)
     for n in range(len(PAIRS)):
-        row = row + jnp.where(lane == n, jnp.sum(jnp.sum(acc[n], axis=0, keepdims=True), axis=1, keepdims=True), 0.0)
-    rows_out[...] = jnp.broadcast_to(row, (NDEV, HZ))
+        row = row + jnp.where(lane1 == n, total_of(jnp.sum(acc[n], axis=0, keepdims=True)), 0.0)
+    payload = words[...]
+    both = jnp.concatenate([payload, pltpu.roll(payload, W_NEXT, 1)], axis=0)
+    rows_out[...] = pick(table[...], both) + row
     mine = exchange_start(rows_out, rows_in, lsem.at[8], asem.at[0], asem.at[1])
+    edge.wait()
+
+    @pl.when(me == 0)
+    def _():
+        over[:, 0:1, :] = jnp.zeros((3, 1, HZ), jnp.float32)
+
     exchange_wait(mine, rows_out, rows_in, asem.at[0], asem.at[1])
-    total = jnp.sum(rows_in[...], axis=0, keepdims=True)
+    got = rows_in[...]
+    total = jnp.sum(got, axis=0, keepdims=True)
     gram = {}
     for n, key in enumerate(PAIRS):
-        gram[key] = jnp.broadcast_to(jnp.sum(jnp.where(lane == n, total, 0.0), axis=1, keepdims=True), (1, HZ))
+        gram[key] = jnp.broadcast_to(total_of(jnp.where(lane1 == n, total, 0.0)), (1, HZ))
     coef, worst = iterate(lambda i, j: gram[(i, j)])
     flag_ref[...] = jnp.broadcast_to(worst, (8, HZ))
+
+    words[...] = jnp.transpose(got)
+    lefts, lefts2, rights, rights2 = [], [], [], []
+    for s in (0, 1):
+        at = W_BASIS + s * W_NEXT
+        traction = words[at:at + 3, :]
+        for j in range(4):
+            traction = traction + coef[j] * words[at + 3 * (j + 1):at + 3 * (j + 1) + 3, :]
+        where = words[W_NODE + s * W_NEXT:W_NODE + s * W_NEXT + 1, :].astype(jnp.int32)
+        high, low = where // HZ, where % HZ
+        block = row_of((NBLK, HZ))
+        lefts.append(jnp.concatenate([jnp.where(block == high, traction[c:c + 1], 0.0) for c in range(3)], axis=0))
+        lefts2.append(jnp.concatenate([jnp.where(block == high + 1, traction[c:c + 1], 0.0) for c in range(3)], axis=0))
+        right = right2 = jnp.zeros(square, jnp.float32)
+        for j in range(RBFW):
+            w = words[W_WEIGHT + s * W_NEXT + j:W_WEIGHT + s * W_NEXT + j + 1, :]
+            right = jnp.where(row_of(square) == low + j, w, right)
+            right2 = jnp.where(row_of(square) + HZ == low + j, w, right2)
+        rights.append(right)
+        rights2.append(right2)
+    applied = lax.dot_general(
+        jnp.concatenate(lefts + lefts2, axis=1), jnp.concatenate(rights + rights2, axis=1),
+        (((1,), (1,)), ((), ())), precision=lax.Precision.HIGHEST, preferred_element_type=jnp.float32)
+    for c in range(3):
+        net = own[c] + over[c, 0:NBLK, :]
+        moved = mass[...] * (applied[c * NBLK:(c + 1) * NBLK] - net)
+        nodal[c, 0:NBLK, :] = moved
+        nodal[c, NBLK:NBLK + 8, :] = jnp.zeros((8, HZ), jnp.float32)
+        force[c] = disp[c, 0:NBLK, :] + SHELL_STEP * moved
+    near = jnp.concatenate([nodal[c, 0:NBLK, :] for c in range(3)] + [nodal[c, 1:NBLK + 1, :] for c in range(3)], axis=1)
+    stack = jnp.concatenate(thirds(near), axis=0)
+    result = jnp.zeros(square, jnp.float32)
+    for s in (0, 1):
+        where = got[:, W_NODE + s * W_NEXT:W_NODE + s * W_NEXT + 1].astype(jnp.int32)
+        high, low = where // HZ, where % HZ
+        block = lax.rem(lane_of((HZ, 3 * NBLK)), NBLK)
+        chosen = jnp.where(block == high, 1.0, 0.0).astype(jnp.bfloat16)
+        vals = jnp.dot(chosen, stack, preferred_element_type=jnp.float32)
+        here = there = jnp.zeros(square, jnp.float32)
+        for j in range(RBFW):
+            w = got[:, W_WEIGHT + s * W_NEXT + j:W_WEIGHT + s * W_NEXT + j + 1]
+            here = jnp.where(lane == low + j, w, here)
+            there = jnp.where(lane + HZ == low + j, w, there)
+        for c in range(3):
+            v = total_of(vals[:, c * HZ:(c + 1) * HZ] * here + vals[:, (3 + c) * HZ:(4 + c) * HZ] * there)
+            result = jnp.where(lane == 3 * s + c, v, result)
+    back_out[...] = result
+    mine = exchange_start(back_out, back_in, lsem.at[8], asem.at[2], asem.at[3])
 
     def combine(region):
         res = None
@@ -406,8 +675,8 @@
     def correct(region):
         _, sides = pairs_of(region, press)
         for c in range(3):
-            own = region.get(pred.at[SLOT[c]])
-            new = each(lambda v, a, b: v - 0.5 * (a - b), own, sides[c][0], sides[c][1])
+            prior = region.get(pred.at[SLOT[c]])
+            new = each(lambda v, a, b: v - 0.5 * (a - b), prior, sides[c][0], sides[c][1])
             for h in (0, 1):
                 nvel[c, region.x - OX, h, region.y - OY:region.y - OY + region.n, :] = new[h]
 
@@ -420,116 +689,72 @@
             press.at[OX:OX + CX, h, OY:OY + CY, :], p_hbm.at[:, :, z], lsem.at[2 * h + 1]))
     for cp in stores:
         cp.start()
+    for b in range(NBLK):
+        disp_out[:, b * HZ:(b + 1) * HZ] = force.reshape(12 * NBLK, HZ)[pl.ds(b, 3, stride=NBLK), :]
+    exchange_wait(mine, back_out, back_in, asem.at[2], asem.at[3])
+    answers = jnp.transpose(back_in[...])[0:8]
+    answers = jnp.concatenate(thirds(answers), axis=0)
+    found = [jnp.dot(answers, table[:, s * HZ:(s + 1) * HZ], preferred_element_type=jnp.float32) for s in (0, 1)]
+    found = [f[0:8] + f[8:16] + f[16:24] for f in found]
+    iface_out[...] = found[0][0:3] + found[1][3:6]
     for cp in stores:
         cp.wait()
 
 
-def fluid(velocity, damping):
+def local(velocity, damping, displacement, stiffness, connectivity, inv_mass, iface_cell, iface_owner, iface_node,
+          rbf_weight, normals):
     field = (PX, 2, PY, HZ)
-    f32 = jnp.float32
+    f32, i32 = jnp.float32, jnp.int32
     anywhere = pl.BlockSpec(memory_space=pl.ANY)
-    return pl.pallas_call(
-        fluid_kernel,
+    vmem = pl.BlockSpec(memory_space=pltpu.VMEM)
+    smem = pl.BlockSpec(memory_space=pltpu.SMEM)
+    square = pltpu.VMEM((HZ, HZ), f32)
+    outs = pl.pallas_call(
+        step_kernel,
         out_shape=(
             jax.ShapeDtypeStruct(velocity.shape, f32),
             jax.ShapeDtypeStruct(damping.shape, f32),
+            jax.ShapeDtypeStruct(displacement.shape, f32),
+            jax.ShapeDtypeStruct(normals.shape, f32),
             jax.ShapeDtypeStruct((8, HZ), f32),
         ),
-        in_specs=[anywhere] * 2,
-        out_specs=(anywhere, anywhere, pl.BlockSpec(memory_space=pltpu.VMEM)),
+        in_specs=[anywhere] * 3 + [vmem] * 3 + [smem] + [vmem] * 5,
+        out_specs=(anywhere, anywhere, vmem, vmem, vmem),
         scratch_shapes=[
             pltpu.VMEM((3,) + field, f32),
             pltpu.VMEM(field, f32),
             pltpu.VMEM((3,) + field, f32),
-            pltpu.VMEM((4,) + field, f32),
+            pltpu.VMEM(field, f32),
+            pltpu.VMEM(field, f32),
+            pltpu.VMEM(field, f32),
+            pltpu.VMEM(field, f32),
             pltpu.VMEM(field, f32),
             pltpu.VMEM((3, CX, 2, CY, HZ), f32),
-            pltpu.VMEM((NDEV, HZ), f32),
-            pltpu.VMEM((NDEV, HZ), f32),
+            pltpu.VMEM((12, 12, NBLK * HZ), f32),
+            pltpu.VMEM((3, 40, HZ), f32),
+            pltpu.VMEM((4, NBLK, HZ), i32),
+            pltpu.VMEM((NBLK * 16, HZ), f32),
+            pltpu.VMEM((12, NBLK, HZ), f32),
+            pltpu.VMEM((3, NBLK, HZ), f32),
+            pltpu.VMEM((3, 40, HZ), f32),
+            square, square, square, square, square,
+            pltpu.VMEM((HZ, 2 * HZ), jnp.bfloat16),
+            pltpu.VMEM((3, 40, HZ), f32),
+            square, square, square, square,
             pltpu.SemaphoreType.DMA((9,)),
-            pltpu.SemaphoreType.DMA((32,)),
-            pltpu.SemaphoreType.DMA((32,)),
-            pltpu.SemaphoreType.DMA((2,)),
+            pltpu.SemaphoreType.DMA((4,)),
+            pltpu.SemaphoreType.DMA((34,)),
+            pltpu.SemaphoreType.DMA((34,)),
+            pltpu.SemaphoreType.DMA((4,)),
         ],
         compiler_params=pltpu.CompilerParams(
-            collective_id=0, has_side_effects=True, vmem_limit_bytes=48 << 20),
-        name="fluid",
-    )(velocity, damping)
-
-
-RIM = 64
-RBFW = 4
-WALL_FRICTION = 0.5
-SHELL_STEP = 0.5
-
-
-def from_behind(value, axis, steps):
-    count = lax.axis_size(axis)
-    leading, last = (max(0, -steps), min(count, count - steps))
-    return lax.ppermute(value, axis, [(source, source + steps) for source in range(leading, last)])
-
-
-def local(
-    velocity,
-    damping,
-    displacement,
-    stiffness,
-    connectivity,
-    inv_mass,
-    iface_cell,
-    iface_owner,
-    iface_node,
-    rbf_weight,
-    normals,
-):
-    shell_nodes = displacement.shape[1]
-    rim_values = from_behind(displacement[:, :RIM], ("grp", "dom"), -1)
-    extended_disp = jnp.concatenate([displacement, rim_values], axis=1)
-    element_count = connectivity.shape[1]
-    corner_values = extended_disp[:, connectivity]
-    element_dofs = jnp.transpose(corner_values, (1, 0, 2)).reshape(12, element_count)
-    element_force = jnp.sum(stiffness * element_dofs[None], axis=1).reshape(4, 3, element_count)
-    node_force = jnp.zeros((3, shell_nodes + RIM), jnp.float32)
-    for corner in range(4):
-        node_force = node_force.at[:, connectivity[corner]].add(element_force[corner])
-    rim_force = from_behind(node_force[:, shell_nodes:], ("grp", "dom"), 1)
-    stiff_force = node_force[:, :shell_nodes] + jnp.pad(rim_force, ((0, 0), (0, shell_nodes - RIM)))
-    new_velocity, pressure, _ = fluid(velocity, damping)
-    pressure_at = pressure.reshape(-1)[iface_cell]
-    velocity_at = new_velocity.reshape(3, -1)[:, iface_cell]
-    traction = -pressure_at[None] * normals + WALL_FRICTION * velocity_at
-    owner_dev = iface_owner[:, 0]
-    point_count = owner_dev.shape[0]
-    devices = lax.axis_size("grp") * lax.axis_size("dom")
-    owner_cap = max(2, 2 * point_count // devices)
-    order_index = lax.iota(jnp.int32, point_count)
-    earlier = (owner_dev[None, :] == owner_dev[:, None]) & (
-        order_index[None, :] < order_index[:, None]
+            collective_id=0, has_side_effects=True, vmem_limit_bytes=60 << 20),
+        name="step",
+    )(
+        velocity, damping, stiffness, displacement, connectivity, inv_mass.reshape(NBLK, HZ), iface_cell,
+        iface_cell.reshape(1, NPTS), iface_owner.reshape(1, NPTS), iface_node.reshape(1, NPTS), rbf_weight, normals,
     )
-    slot_rank = jnp.sum(earlier.astype(jnp.int32), axis=1)
-    slot_index = owner_dev * owner_cap + slot_rank
-    slot_count = devices * owner_cap
-    payload = jnp.concatenate([traction, rbf_weight, iface_node.astype(jnp.float32)[None]], axis=0)
-    outgoing = jnp.zeros((payload.shape[0], slot_count), jnp.float32).at[:, slot_index].set(payload)
-    received = lax.all_to_all(outgoing, ("grp", "dom"), split_axis=1, concat_axis=1, tiled=True)
-    slot_traction = received[:3]
-    slot_weight = received[3 : 3 + RBFW]
-    slot_node = received[3 + RBFW].astype(jnp.int32)
-    applied = jnp.zeros((3, shell_nodes), jnp.float32)
-    for offset in range(RBFW):
-        applied = applied.at[:, slot_node + offset].add(slot_weight[offset][None] * slot_traction)
-    node_velocity = inv_mass[None] * (applied - stiff_force)
-    new_displacement = displacement + SHELL_STEP * node_velocity
-    slot_velocity = jnp.zeros((3, slot_count), jnp.float32)
-    for offset in range(RBFW):
-        slot_velocity = (
-            slot_velocity + slot_weight[offset][None] * node_velocity[:, slot_node + offset]
-        )
-    returned_vals = lax.all_to_all(
-        slot_velocity, ("grp", "dom"), split_axis=1, concat_axis=1, tiled=True
-    )
-    iface_velocity = returned_vals[:, slot_index]
-    return (new_velocity, pressure, new_displacement, iface_velocity)
+    return outs[:4]
 
 
 def solution(mesh):

time: 335 us -> 62.4 us (0.19)
  local copies, waits for them, and re-layouts: 132 us -> 4.8 us
  other arithmetic: 122 us -> 0 us
  starting transfers between devices: 27.3 us -> 0 us
  Pallas kernels: 44.2 us -> 56.7 us
  waiting for transfers between devices: 7.1 us -> 0 us
    scatter-add x8 -> x0, other arithmetic: 111 us -> none  [the longest x4 94.1 us: local(): node_force.at[:, connectivity[corner]].add(element_force[corner])]
    gather x9 -> x0, local copies, waits for them, and re-layouts: 74.1 us -> none  [the longest x2 61.3 us: local(): corner_values = extended_disp[:, connectivity]]
    reshape x1 -> x0, local copies, waits for them, and re-layouts: 32.4 us -> none  [local(): velocity_at = new_velocity.reshape(3, -1)[:, iface_cell]]
    all_to_all x2 -> x0, starting transfers between devices: 21.8 us -> none  [the longest x1 13.4 us: local(): lax.all_to_all(slot_velocity, ('grp', 'dom'), split_axis=1, concat_axis=1...]
    pallas_call x1, Pallas kernels: 44.2 us -> 56.7 us  [local(): pl.pallas_call(step_kernel, out_shape=(jax.ShapeDtypeStruct(velocity.shap...]
    slice x13 -> x0, local copies, waits for them, and re-layouts: 10.3 us -> none  [the longest x5 7.98 us: local(): element_force[corner]]
    all_to_all x2 -> x0, waiting for transfers between devices: 6.97 us -> none  [the longest x1 6.97 us: local(): lax.all_to_all(slot_velocity, ('grp', 'dom'), split_axis=1, concat_axis=1...]
    add x3 -> x0, other arithmetic: 5.72 us -> none  [the longest x1 4.44 us: local(): new_displacement = displacement + SHELL_STEP * node_velocity]
  transfers between devices with their start and end apart: 4 -> 0, of which waited for: 2 -> 0; matrix products, arithmetic and copies ran while one was open for 59% -> 0% of each run, Pallas kernels for 0% -> 0%
where the time goes in v2:
time: 62.4 us; the launch traced here: 62.2 us
  Pallas kernels  56.7 us (91%)
  local copies, waits for them, and re-layouts  4.8 us (8%)
  between operations  0.67 us (1%)
    pallas_call x1, Pallas kernels, local(): pl.pallas_call(step_kernel, out_shape=(jax.ShapeDtypeStruct(velocity.shap...  56.7 us
    unnamed x10, local copies, waits for them, and re-layouts  4.8 us

profile of v2, /device:TPU:1, one launch (start us, length us, event | category | flops | bytes accessed | tf_op | source)
XLA Modules:
  0.0 62.2 jit_solution(14937147981347168836)
XLA Ops:
  0.6 56.7 %step.1 = (f32[3,16,32,256]{3,2,1,0:T(8,128)}, f32[16,32,256]{2,1,0:T(8,128)}, f32[3,4096]{1,0:T(4,128)}, f32[3,128]{1,0:T(4,128)}, f32[8,128]{1,0:T(8,128)}) custom-call(f32[3,16,32,256]{3,2,1,0:T(8,128)} %vel_hbm.1, f32[16,32,256]{2,1,0:T(8,128)} %damp_hbm.1, f32[12,12,4096]{2,1,0:T(8,128)} %stiff_hbm.1, f32[3,4096]{1,0:T(4,128)} %disp_in.1, ...), custom_call_target="tpu_custom_call" | custom-call | tf_op jit(solution)/shard_map/step/pallas_call | solution.py:712
  57.4 0.0 copy-start
  57.4 0.0 copy-start.1
  57.4 0.0 copy-start.2
  57.4 2.8 %copy.19 = f32[3,16,32,256]{3,2,1,0:T(8,128)} copy(f32[3,16,32,256]{3,2,1,0:T(8,128)} %get-tuple-element.16) | data formatting | bytes 3145728
  60.2 0.0 copy-done
  60.2 0.8 %copy.20 = f32[16,32,256]{2,1,0:T(8,128)} copy(f32[16,32,256]{2,1,0:T(8,128)S(1)} %copy-done) | data formatting | bytes 1048576
  61.0 0.0 copy-done.1
  61.0 0.6 %copy.21 = f32[3,4096]{1,0:T(4,128)} copy(f32[3,4096]{1,0:T(4,128)S(1)} %copy-done.1) | data formatting | bytes 98304
  61.6 0.0 copy-done.2
  61.6 0.6 copy.22
Async XLA Ops:
  57.4 2.8 %copy-start = (f32[16,32,256]{2,1,0:T(8,128)S(1)}, f32[16,32,256]{2,1,0:T(8,128)}, u32[]{:S(2)}) copy-start(f32[16,32,256]{2,1,0:T(8,128)} %get-tuple-element.17) | copy-start | bytes 1572868
  57.4 3.6 %copy-start.1 = (f32[3,4096]{1,0:T(4,128)S(1)}, f32[3,4096]{1,0:T(4,128)}, u32[]{:S(2)}) copy-start(f32[3,4096]{1,0:T(4,128)} %get-tuple-element.18) | copy-start | bytes 147460
  57.4 4.2 %copy-start.2 = (f32[3,128]{1,0:T(4,128)S(1)}, f32[3,128]{1,0:T(4,128)}, u32[]{:S(2)}) copy-start(f32[3,128]{1,0:T(4,128)} %get-tuple-element.19) | copy-start | bytes 4612

commit v3 on v2

--- a/solution.py
+++ b/solution.py
@@ -119,13 +119,13 @@
     return res
 
 
-def all_planes(fn, lo=OX, hi=OX + CX, parts=2):
+def all_planes(fn, lo=OX, hi=OX + CX, parts=2, unroll=2):
     def body(x, carry):
         for k in range(parts):
             fn(Plane(x, OY + k * (CY // parts), CY // parts))
         return carry
 
-    lax.fori_loop(lo, hi, body, 0)
+    lax.fori_loop(lo, hi, body, 0, unroll=unroll)
 
 
 def position():
@@ -200,17 +200,21 @@
     return copies
 
 
+def everyone(fn):
+    g, d = position()
+    for dg in range(NGRP):
+        tg = lax.rem(g + dg, NGRP)
+
+        def body(i, carry):
+            fn(tg, lax.rem(d + i, NDOM))
+            return carry
+
+        lax.fori_loop(0 if dg else 1, NDOM, body, 0, unroll=16 if dg else 31)
+
+
 def greet_all():
-    g, d = position()
-    me = g * NDOM + d
     barrier = pltpu.get_barrier_semaphore()
-
-    def body(i, carry):
-        t = lax.rem(me + i, NDEV)
-        pl.semaphore_signal(barrier, inc=1, device_id=(t // NDOM, lax.rem(t, NDOM)), device_id_type=MESH)
-        return carry
-
-    lax.fori_loop(1, NDEV, body, 0, unroll=8)
+    everyone(lambda tg, td: pl.semaphore_signal(barrier, inc=1, device_id=(tg, td), device_id_type=MESH))
     return barrier
 
 
@@ -219,17 +223,10 @@
     me = g * NDOM + d
     mine = pltpu.make_async_copy(out_ref.at[pl.ds(me, 1)], in_ref.at[pl.ds(me, 1)], own)
     mine.start()
-
-    def body(i, carry):
-        t = lax.rem(me + i, NDEV)
-        pltpu.make_async_remote_copy(
-            src_ref=out_ref.at[pl.ds(t, 1)], dst_ref=in_ref.at[pl.ds(me, 1)],
-            send_sem=send, recv_sem=recv,
-            device_id=(t // NDOM, lax.rem(t, NDOM)), device_id_type=MESH,
-        ).start()
-        return carry
-
-    lax.fori_loop(1, NDEV, body, 0, unroll=8)
+    everyone(lambda tg, td: pltpu.make_async_remote_copy(
+        src_ref=out_ref.at[pl.ds(tg * NDOM + td, 1)], dst_ref=in_ref.at[pl.ds(me, 1)],
+        send_sem=send, recv_sem=recv, device_id=(tg, td), device_id_type=MESH,
+    ).start())
     return mine
 
 
@@ -393,9 +390,7 @@
         for u in range(4):
             k = i * 4 + u
             cell = cells[k]
-            x = lax.div(cell, CY * 2 * HZ) + OX
-            y = lax.rem(lax.div(cell, 2 * HZ), CY) + OY
-            h = lax.rem(lax.div(cell, HZ), 2)
+            x, y, h = (cell >> 13) + OX, ((cell >> 8) & (CY - 1)) + OY, (cell >> 7) & 1
             at = pl.ds(k, 1)
             mid0[at, :] = f[x, 0, pl.ds(y, 1), :]
             mid1[at, :] = f[x, 1, pl.ds(y, 1), :]
@@ -411,9 +406,7 @@
         for u in range(4):
             k = i * 4 + u
             cell = cells[k]
-            x = lax.div(cell, CY * 2 * HZ) + OX
-            y = lax.rem(lax.div(cell, 2 * HZ), CY) + OY
-            h = lax.rem(lax.div(cell, HZ), 2)
+            x, y, h = (cell >> 13) + OX, ((cell >> 8) & (CY - 1)) + OY, (cell >> 7) & 1
             for f, o in zip(fields, outs):
                 o[pl.ds(k, 1), :] = f[x, h, pl.ds(y, 1), :]
         return carry
@@ -454,22 +447,7 @@
 
     spread(disp_in, disp.reshape(3 * 40, HZ), 3, 40)
     spread(conn_in, conn.reshape(4 * NBLK, HZ), 4, NBLK)
-    for q in range(3):
-        shell_gather(q, disp, conn, dofs)
-        blocks[q].wait()
-        shell_product(q, stiff, dofs, force)
-
     square = (HZ, HZ)
-    owns = owner[...] == row_of(square)
-    first = jnp.min(jnp.where(owns, lane_of(square), HZ), axis=1, keepdims=True)
-    for s in (0, 1):
-        table[:, s * HZ:(s + 1) * HZ] = jnp.where(
-            owns & ((lane_of(square) == first) == (s == 0)), 1.0, 0.0).astype(jnp.bfloat16)
-    words[...] = jnp.zeros(square, jnp.float32)
-    words[W_WEIGHT:W_WEIGHT + 4, :] = weight[...]
-    words[W_NODE:W_NODE + 1, :] = node[...].astype(jnp.float32)
-    words[...] = jnp.transpose(words[...])
-
     for cp in loads[:8]:
         cp.wait()
     pl.semaphore_wait(barrier, NDEV - 1)
@@ -487,7 +465,9 @@
         device_id=(lax.div(before, NDOM), lax.rem(before, NDOM)), device_id_type=MESH)
     rim.start()
     for q in range(3):
-        shell_scatter(q, conn, force, own, over)
+        shell_gather(q, disp, conn, dofs)
+        blocks[q].wait()
+        shell_product(q, stiff, dofs, force)
     for cp in copies:
         cp.wait()
     for c in range(3):
@@ -539,6 +519,7 @@
         src_ref=over.at[:, NBLK:NBLK + 1, :], dst_ref=over.at[:, 0:1, :], send_sem=ssem.at[33], recv_sem=rsem.at[33],
         device_id=(lax.div(after, NDOM), lax.rem(after, NDOM)), device_id_type=MESH)
     edge.start()
+    shell_scatter(0, conn, force, own, over)
     for cp in moving:
         cp.wait()
     clear_outside(t0)
@@ -546,6 +527,15 @@
     all_planes(lambda region: cheb(region, damp, t1, t0, t2))
 
     moving = swap(t2, 24)
+    owns = owner[...] == row_of(square)
+    first = jnp.min(jnp.where(owns, lane_of(square), HZ), axis=1, keepdims=True)
+    for s in (0, 1):
+        table[:, s * HZ:(s + 1) * HZ] = jnp.where(
+            owns & ((lane_of(square) == first) == (s == 0)), 1.0, 0.0).astype(jnp.bfloat16)
+    words[...] = jnp.zeros(square, jnp.float32)
+    words[W_WEIGHT:W_WEIGHT + 4, :] = weight[...]
+    words[W_NODE:W_NODE + 1, :] = node[...].astype(jnp.float32)
+    words[...] = jnp.transpose(words[...])
     z_all = column(cell_row[...]) & (2 * HZ - 1)
     lane = lane_of(square)
     hit0, hit1 = lane == z_all, lane + HZ == z_all
@@ -598,6 +588,8 @@
     both = jnp.concatenate([payload, pltpu.roll(payload, W_NEXT, 1)], axis=0)
     rows_out[...] = pick(table[...], both) + row
     mine = exchange_start(rows_out, rows_in, lsem.at[8], asem.at[0], asem.at[1])
+    shell_scatter(1, conn, force, own, over)
+    shell_scatter(2, conn, force, own, over)
     edge.wait()
 
     @pl.when(me == 0)
@@ -611,7 +603,7 @@
     for n, key in enumerate(PAIRS):
         gram[key] = jnp.broadcast_to(total_of(jnp.where(lane1 == n, total, 0.0)), (1, HZ))
     coef, worst = iterate(lambda i, j: gram[(i, j)])
-    flag_ref[...] = jnp.broadcast_to(worst, (8, HZ))
+    flag_ref[0, 0] = jnp.where(worst > GUARD, 1, 0).astype(jnp.int32)[0, 0]
 
     words[...] = jnp.transpose(got)
     lefts, lefts2, rights, rights2 = [], [], [], []
@@ -701,7 +693,7 @@
         cp.wait()
 
 
-def local(velocity, damping, displacement, stiffness, connectivity, inv_mass, iface_cell, iface_owner, iface_node,
+def fused(velocity, damping, displacement, stiffness, connectivity, inv_mass, iface_cell, iface_owner, iface_node,
           rbf_weight, normals):
     field = (PX, 2, PY, HZ)
     f32, i32 = jnp.float32, jnp.int32
@@ -716,10 +708,10 @@
             jax.ShapeDtypeStruct(damping.shape, f32),
             jax.ShapeDtypeStruct(displacement.shape, f32),
             jax.ShapeDtypeStruct(normals.shape, f32),
-            jax.ShapeDtypeStruct((8, HZ), f32),
+            jax.ShapeDtypeStruct((1, 1), i32),
         ),
         in_specs=[anywhere] * 3 + [vmem] * 3 + [smem] + [vmem] * 5,
-        out_specs=(anywhere, anywhere, vmem, vmem, vmem),
+        out_specs=(anywhere, anywhere, vmem, vmem, smem),
         scratch_shapes=[
             pltpu.VMEM((3,) + field, f32),
             pltpu.VMEM(field, f32),
@@ -754,7 +746,223 @@
         velocity, damping, stiffness, displacement, connectivity, inv_mass.reshape(NBLK, HZ), iface_cell,
         iface_cell.reshape(1, NPTS), iface_owner.reshape(1, NPTS), iface_node.reshape(1, NPTS), rbf_weight, normals,
     )
-    return outs[:4]
+    return outs
+
+
+ITERS = 4
+VISCOSITY = 1.0
+GUARD = 4e-4
+UNIT_STEPS = ((1, 0, 0), (0, 1, 0), (0, 0, 1))
+
+
+def with_halo(block, sides, width):
+    for axis, dim in sides:
+        count = lax.axis_size(axis)
+        forward = [(i, i + 1) for i in range(count - 1)]
+        backward = [(target, source) for source, target in forward]
+        low = lax.ppermute(
+            lax.slice_in_dim(block, block.shape[dim] - width, None, axis=dim), axis, forward
+        )
+        high = lax.ppermute(lax.slice_in_dim(block, 0, width, axis=dim), axis, backward)
+        block = jnp.concatenate([low, block, high], axis=dim)
+    return block
+
+
+def from_behind(value, axis, steps):
+    count = lax.axis_size(axis)
+    leading, last = (max(0, -steps), min(count, count - steps))
+    return lax.ppermute(value, axis, [(source, source + steps) for source in range(leading, last)])
+
+
+def window_at(padded, offsets):
+    size_x = padded.shape[-3] - 2
+    size_y = padded.shape[-2] - 2
+    size_z = padded.shape[-1] - 2
+    return padded[
+        ...,
+        1 + offsets[0] : 1 + offsets[0] + size_x,
+        1 + offsets[1] : 1 + offsets[1] + size_y,
+        1 + offsets[2] : 1 + offsets[2] + size_z,
+    ]
+
+
+def backward(unit_step):
+    return tuple((-value for value in unit_step))
+
+
+def pad_depth(source):
+    spec = [(0, 0)] * (source.ndim - 1) + [(1, 1)]
+    return jnp.pad(source, spec)
+
+
+def predictor(padded):
+    centre = window_at(padded, (0, 0, 0))
+    laplace = -6.0 * centre
+    advect = jnp.zeros_like(centre)
+    for axis_num, unit_step in enumerate(UNIT_STEPS):
+        forward = window_at(padded, unit_step)
+        behind_cells = window_at(padded, backward(unit_step))
+        laplace = laplace + forward + behind_cells
+        advect = advect + centre[axis_num : axis_num + 1] * (0.5 * (forward - behind_cells))
+    return centre + TIME_STEP * (VISCOSITY * laplace - advect)
+
+
+def divergence(padded):
+    summed = jnp.zeros(window_at(padded[0], (0, 0, 0)).shape, jnp.float32)
+    for axis_num, unit_step in enumerate(UNIT_STEPS):
+        component = padded[axis_num]
+        summed = summed + 0.5 * (
+            window_at(component, unit_step) - window_at(component, backward(unit_step))
+        )
+    return -summed
+
+
+def padded_cells(source):
+    extended = with_halo(source, (("grp", 0), ("dom", 1)), 1)
+    return pad_depth(extended)
+
+
+def operate(source, damping):
+    padded = padded_cells(source)
+    centre = window_at(padded, (0, 0, 0))
+    beside = jnp.zeros_like(centre)
+    for unit_step in UNIT_STEPS:
+        beside = beside + window_at(padded, unit_step) + window_at(padded, backward(unit_step))
+    return (6.0 + damping) * centre - beside
+
+
+def squares(residual):
+    return lax.psum(jnp.sum(residual * residual), ("grp", "dom"))
+
+
+def plain(
+    velocity,
+    damping,
+    displacement,
+    stiffness,
+    connectivity,
+    inv_mass,
+    iface_cell,
+    iface_owner,
+    iface_node,
+    rbf_weight,
+    normals,
+):
+    shell_nodes = displacement.shape[1]
+    rim_values = from_behind(displacement[:, :RIM], ("grp", "dom"), -1)
+    extended_disp = jnp.concatenate([displacement, rim_values], axis=1)
+    element_count = connectivity.shape[1]
+    corner_values = extended_disp[:, connectivity]
+    element_dofs = jnp.transpose(corner_values, (1, 0, 2)).reshape(12, element_count)
+    element_force = jnp.sum(stiffness * element_dofs[None], axis=1).reshape(4, 3, element_count)
+    node_force = jnp.zeros((3, shell_nodes + RIM), jnp.float32)
+    for corner in range(4):
+        node_force = node_force.at[:, connectivity[corner]].add(element_force[corner])
+    rim_force = from_behind(node_force[:, shell_nodes:], ("grp", "dom"), 1)
+    stiff_force = node_force[:, :shell_nodes] + jnp.pad(rim_force, ((0, 0), (0, shell_nodes - RIM)))
+    extended = with_halo(velocity, (("grp", 1), ("dom", 2)), 1)
+    predicted = predictor(pad_depth(extended))
+    star_wide = with_halo(predicted, (("grp", 1), ("dom", 2)), 1)
+    star_padded = pad_depth(star_wide)
+    right_side = divergence(star_padded)
+    pressure = jnp.zeros_like(right_side)
+    residual = right_side
+    direction = right_side
+    norm_now = squares(residual)
+    for sweep in range(ITERS):
+        mapped = operate(direction, damping)
+        step_size = norm_now / lax.psum(jnp.sum(direction * mapped), ("grp", "dom"))
+        pressure = pressure + step_size * direction
+        residual = residual - step_size * mapped
+        norm_next = squares(residual)
+        direction = residual + norm_next / norm_now * direction
+        norm_now = norm_next
+    pressure_wide = padded_cells(pressure)
+    new_velocity = predicted - jnp.stack(
+        [
+            0.5
+            * (window_at(pressure_wide, unit_step) - window_at(pressure_wide, backward(unit_step)))
+            for unit_step in UNIT_STEPS
+        ]
+    )
+    pressure_at = pressure.reshape(-1)[iface_cell]
+    velocity_at = new_velocity.reshape(3, -1)[:, iface_cell]
+    traction = -pressure_at[None] * normals + WALL_FRICTION * velocity_at
+    owner_dev = iface_owner[:, 0]
+    point_count = owner_dev.shape[0]
+    devices = lax.axis_size("grp") * lax.axis_size("dom")
+    owner_cap = max(2, 2 * point_count // devices)
+    order_index = lax.iota(jnp.int32, point_count)
+    earlier = (owner_dev[None, :] == owner_dev[:, None]) & (
+        order_index[None, :] < order_index[:, None]
+    )
+    slot_rank = jnp.sum(earlier.astype(jnp.int32), axis=1)
+    slot_index = owner_dev * owner_cap + slot_rank
+    slot_count = devices * owner_cap
+    payload = jnp.concatenate([traction, rbf_weight, iface_node.astype(jnp.float32)[None]], axis=0)
+    outgoing = jnp.zeros((payload.shape[0], slot_count), jnp.float32).at[:, slot_index].set(payload)
+    received = lax.all_to_all(outgoing, ("grp", "dom"), split_axis=1, concat_axis=1, tiled=True)
+    slot_traction = received[:3]
+    slot_weight = received[3 : 3 + RBFW]
+    slot_node = received[3 + RBFW].astype(jnp.int32)
+    applied = jnp.zeros((3, shell_nodes), jnp.float32)
+    for offset in range(RBFW):
+        applied = applied.at[:, slot_node + offset].add(slot_weight[offset][None] * slot_traction)
+    node_velocity = inv_mass[None] * (applied - stiff_force)
+    new_displacement = displacement + SHELL_STEP * node_velocity
+    slot_velocity = jnp.zeros((3, slot_count), jnp.float32)
+    for offset in range(RBFW):
+        slot_velocity = (
+            slot_velocity + slot_weight[offset][None] * node_velocity[:, slot_node + offset]
+        )
+    returned_vals = lax.all_to_all(
+        slot_velocity, ("grp", "dom"), split_axis=1, concat_axis=1, tiled=True
+    )
+    iface_velocity = returned_vals[:, slot_index]
+    return (new_velocity, pressure, new_displacement, iface_velocity)
+
+
+def relay_kernel(*refs):
+    count = (len(refs) - 2) // 3
+    ins, outs, held = refs[:count], refs[count:2 * count], refs[2 * count:3 * count]
+    come, go = refs[-2:]
+    pieces = []
+    for a, b, c in zip(ins, outs, held):
+        if len(a.shape) > 2:
+            pieces += [(a.at[k], b.at[k], c.at[k]) for k in range(a.shape[0])]
+        else:
+            pieces.append((a, b, c))
+    arrive = [pltpu.make_async_copy(a, c, come.at[n]) for n, (a, b, c) in enumerate(pieces)]
+    leave = [pltpu.make_async_copy(c, b, go.at[n]) for n, (a, b, c) in enumerate(pieces)]
+    for cp in arrive:
+        cp.start()
+    for x, y in zip(arrive, leave):
+        x.wait()
+        y.start()
+    for y in leave:
+        y.wait()
+
+
+def relay(new_velocity, pressure, new_displacement, iface_velocity):
+    arrays = (new_velocity, pressure.reshape(4, CX // 4, CY, 2 * HZ), new_displacement, iface_velocity)
+    anywhere = pl.BlockSpec(memory_space=pl.ANY)
+    count = 3 + 4 + 2
+    outs = pl.pallas_call(
+        relay_kernel,
+        out_shape=tuple(jax.ShapeDtypeStruct(a.shape, a.dtype) for a in arrays),
+        in_specs=[anywhere] * len(arrays),
+        out_specs=(anywhere,) * len(arrays),
+        scratch_shapes=[pltpu.VMEM(a.shape, a.dtype) for a in arrays]
+        + [pltpu.SemaphoreType.DMA((count,)), pltpu.SemaphoreType.DMA((count,))],
+        compiler_params=pltpu.CompilerParams(vmem_limit_bytes=60 << 20),
+        name="relay",
+    )(*arrays)
+    return outs[0], outs[1].reshape(pressure.shape), outs[2], outs[3]
+
+
+def local(*args):
+    *outs, sound = fused(*args)
+    return lax.cond(sound.reshape(()) > 0, lambda: relay(*outs), lambda: plain(*args))
 
 
 def solution(mesh):

time: 62.4 us -> 57 us (0.913)
  local copies, waits for them, and re-layouts: 4.8 us -> 0.64 us
  Pallas kernels: 56.7 us -> 54.6 us
  between operations: 0.67 us -> 1.32 us
    unnamed x10 -> x14, local copies, waits for them, and re-layouts: 4.8 us -> 0.64 us
    pallas_call x1 -> x2, Pallas kernels: 56.7 us -> 54.6 us  [the longest x1 52.1 us: fused(): pl.pallas_call(step_kernel, out_shape=(jax.ShapeDtypeStruct(velocity.shap...]
where the time goes in v3:
time: 57 us; the launch traced here: 56.8 us
  Pallas kernels  54.6 us (96%)
  between operations  1.32 us (2%)
  local copies, waits for them, and re-layouts  0.64 us (1%)
    pallas_call x1, Pallas kernels, fused(): pl.pallas_call(step_kernel, out_shape=(jax.ShapeDtypeStruct(velocity.shap...  52.1 us
    pallas_call x1, Pallas kernels, relay(): pl.pallas_call(relay_kernel, out_shape=tuple((jax.ShapeDtypeStruct(a.shap...  2.51 us

profile of v3, /device:TPU:1, one launch (start us, length us, event | category | flops | bytes accessed | tf_op | source)
XLA Modules:
  0.0 56.8 jit_solution(7713673980705402555)
XLA Ops:
  0.6 0.0 copy-start
  0.6 0.0 copy-start.5
  0.7 0.0 copy-start.12
  0.7 0.0 copy-start.13
  0.7 0.0 copy-start.14
  0.7 52.1 %step.1 = (f32[3,16,32,256]{3,2,1,0:T(8,128)}, f32[16,32,256]{2,1,0:T(8,128)}, f32[3,4096]{1,0:T(4,128)}, f32[3,128]{1,0:T(4,128)}, s32[1,1]{1,0:T(1,128)}) custom-call(f32[3,16,32,256]{3,2,1,0:T(8,128)} %vel_hbm.1, f32[16,32,256]{2,1,0:T(8,128)} %damp_hbm.1, f32[12,12,4096]{2,1,0:T(8,128)} %stiff_hbm.1, f32[3,4096]{1,0:T(4,128)} %disp_in.1, ...), custom_call_target="tpu_custom_call" | custom-call | tf_op jit(solution)/shard_map/step/pallas_call | solution.py:704
  53.4 0.0 copy-done
  53.4 0.0 copy-done.5
  53.4 0.0 copy-done.12
  53.4 0.0 copy-done.13
  53.4 0.0 copy-done.14
  53.4 2.7 %conditional.1 = (f32[16,32,256]{2,1,0:T(8,128)}, f32[3,16,32,256]{3,2,1,0:T(8,128)}, f32[3,4096]{1,0:T(4,128)S(1)}, f32[3,128]{1,0:T(4,128)S(1)}) conditional(s32[]{:T(128)} %bitcast.64, (f32[3,16,32,256]{3,2,1,0:T(8,128)S(1)}, f32[16,32,256]{2,1,0:T(8,128)S(1)}, f32[4096]{0:T(1024)S(1)}, s32[128,1]{0,1:T(1,128)}, s32[128]{0:T(128)}, ...), branch_computations={%region_0.28_spmd, %region_28.29_spmd} | conditional | flops 47965312 | bytes 115600280 | solution.py:965
  53.7 2.5 %relay.1 = (f32[3,16,32,256]{3,2,1,0:T(8,128)}, f32[4,4,32,256]{3,2,1,0:T(8,128)}, f32[3,4096]{1,0:T(4,128)S(1)}, f32[3,128]{1,0:T(4,128)S(1)}) custom-call(f32[3,16,32,256]{3,2,1,0:T(8,128)} %get-tuple-element.41.refs_0_, f32[4,4,32,256]{3,2,1,0:T(8,128)} %bitcast.105, f32[3,4096]{1,0:T(4,128)} %get-tuple-element.43.refs_2_, f32[3,128]{1,0:T(4,128)} %get-tuple-element.44.refs_3_), custom_call_target="tpu_custom_call" | custom-call | tf_op jit(solution)/shard_map/cond/branch_1_fun/relay/pallas_call | solution.py:950
  56.2 0.0 copy-start.18
  56.2 0.0 copy-start.22
  56.2 0.6 %copy-done.18 = f32[3,4096]{1,0:T(4,128)} copy-done((f32[3,4096]{1,0:T(4,128)}, f32[3,4096]{1,0:T(4,128)S(1)}, u32[]{:S(2)}) %copy-start.18) | copy-done | bytes 49176
  56.8 0.0 copy-done.22
Async XLA Ops:
  0.6 52.8 %copy-start = (f32[3,16,32,256]{3,2,1,0:T(8,128)S(1)}, f32[3,16,32,256]{3,2,1,0:T(8,128)}, u32[]{:S(2)}) copy-start(f32[3,16,32,256]{3,2,1,0:T(8,128)} %vel_hbm.1) | copy-start | bytes 4718596
  0.6 52.8 %copy-start.5 = (f32[16,32,256]{2,1,0:T(8,128)S(1)}, f32[16,32,256]{2,1,0:T(8,128)}, u32[]{:S(2)}) copy-start(f32[16,32,256]{2,1,0:T(8,128)} %damp_hbm.1) | copy-start | bytes 1572868
  0.7 52.8 %copy-start.12 = (f32[3,4096]{1,0:T(4,128)S(1)}, f32[3,4096]{1,0:T(4,128)}, u32[]{:S(2)}) copy-start(f32[3,4096]{1,0:T(4,128)} %disp_in.1) | copy-start | bytes 147460
  0.7 52.8 %copy-start.13 = (s32[4,4096]{1,0:T(4,128)S(1)}, s32[4,4096]{1,0:T(4,128)}, u32[]{:S(2)}) copy-start(s32[4,4096]{1,0:T(4,128)} %conn_in.1) | copy-start | bytes 196612
  0.7 52.8 %copy-start.14 = (f32[4096]{0:T(1024)S(1)}, f32[4096]{0:T(1024)}, u32[]{:S(2)}) copy-start(f32[4096]{0:T(1024)} %param.18) | copy-start | bytes 49156
  56.2 0.6 %copy-start.18 = (f32[3,4096]{1,0:T(4,128)}, f32[3,4096]{1,0:T(4,128)S(1)}, u32[]{:S(2)}) copy-start(f32[3,4096]{1,0:T(4,128)S(1)} %get-tuple-element.180) | copy-start | bytes 147460
  56.2 0.6 %copy-start.22 = (f32[3,128]{1,0:T(4,128)}, f32[3,128]{1,0:T(4,128)S(1)}, u32[]{:S(2)}) copy-start(f32[3,128]{1,0:T(4,128)S(1)} %get-tuple-element.181) | copy-start | bytes 4612

commit v4 on v3

--- a/solution.py
+++ b/solution.py
@@ -29,6 +29,22 @@
         self.x, self.y, self.n = x, y, n
 
     def get(self, f, dx=0, dy=0):
+        return [f[self.x + dx, h, self.y + dy:self.y + dy + self.n, :] for h in (0, 1)]
+
+    def put(self, f, halves):
+        for h in (0, 1):
+            f[self.x, h, self.y:self.y + self.n, :] = halves[h]
+
+
+class Inner:
+    def __init__(self, x, k):
+        self.x, self.k, self.n = x, k, CY // 2
+        self.y = OY + k * self.n
+
+    def get(self, f, dx=0, dy=0):
+        if dy == (1 if self.k else -1):
+            own = [f[self.x + dx, h, self.y:self.y + self.n, :] for h in (0, 1)]
+            return [pltpu.roll(v, 1 if dy < 0 else self.n - 1, 0) for v in own]
         return [f[self.x + dx, h, self.y + dy:self.y + dy + self.n, :] for h in (0, 1)]
 
     def put(self, f, halves):
@@ -128,6 +144,25 @@
     lax.fori_loop(lo, hi, body, 0, unroll=unroll)
 
 
+def inner_planes(fn):
+    def body(x, carry):
+        for k in range(2):
+            fn(Inner(x, k))
+        return carry
+
+    lax.fori_loop(OX + 1, OX + CX - 1, body, 0, unroll=2)
+
+
+def edge_planes(fn, out):
+    def body(i, carry):
+        for k in range(2):
+            for base in (OX - out, OX + CX - 1):
+                fn(Plane(base + i, OY + k * (CY // 2), CY // 2))
+        return carry
+
+    lax.fori_loop(0, 1 + out, body, 0, unroll=1 + out)
+
+
 def position():
     return lax.axis_index("grp"), lax.axis_index("dom")
 
@@ -202,20 +237,32 @@
 
 def everyone(fn):
     g, d = position()
-    for dg in range(NGRP):
+    for dg in (2, 1, 3, 0):
         tg = lax.rem(g + dg, NGRP)
 
         def body(i, carry):
             fn(tg, lax.rem(d + i, NDOM))
             return carry
 
-        lax.fori_loop(0 if dg else 1, NDOM, body, 0, unroll=16 if dg else 31)
-
-
-def greet_all():
+        if dg:
+            lax.fori_loop(8, 8 + NDOM, body, 0, unroll=16)
+        else:
+            lax.fori_loop(8, NDOM, body, 0, unroll=12)
+            lax.fori_loop(1, 8, body, 0, unroll=7)
+
+
+def greet_near():
     barrier = pltpu.get_barrier_semaphore()
-    everyone(lambda tg, td: pl.semaphore_signal(barrier, inc=1, device_id=(tg, td), device_id_type=MESH))
+    for dg in (-1, 0, 1):
+        for dd in (-1, 0, 1):
+            if dg or dd:
+                pl.semaphore_signal(barrier, inc=1, device_id=neighbour(dg, dd), device_id_type=MESH)
     return barrier
+
+
+def pass_on(token, reach):
+    for dd in (reach, -reach):
+        pl.semaphore_signal(token, inc=1, device_id=neighbour(0, dd), device_id_type=MESH)
 
 
 def exchange_start(out_ref, in_ref, own, send, recv):
@@ -426,8 +473,8 @@
                 nv_hbm, p_hbm, disp_out, iface_out, flag_ref,
                 vel, damp, pred, t0, t1, t2, t3, press, nvel, stiff,
                 disp, conn, dofs, force, own, over, mid0, mid1, dx, dy, words, table, nodal,
-                rows_out, rows_in, back_out, back_in, lsem, ksem, ssem, rsem, asem):
-    barrier = greet_all()
+                rows_out, rows_in, back_out, back_in, lsem, ksem, ssem, rsem, asem, tokens):
+    barrier = greet_near()
     g, d = position()
     me = g * NDOM + d
     loads = []
@@ -450,7 +497,7 @@
     square = (HZ, HZ)
     for cp in loads[:8]:
         cp.wait()
-    pl.semaphore_wait(barrier, NDEV - 1)
+    pl.semaphore_wait(barrier, 8)
 
     one = slice(None)
     f_x, f_y, f_z = SLOT[0], SLOT[1], SLOT[2]
@@ -458,7 +505,7 @@
     wide_x, wide_y = sides_of(vel, (f_x,), 2)[:2], sides_of(vel, (f_y,), 2)[2:]
     thin_x, thin_y = sides_of(vel, (slice(1, 3),), 1)[:2], sides_of(vel, (slice(0, 2),), 1)[2:]
     copies = start_all(vel, faces + wide_x + wide_y + thin_x + thin_y, ssem, rsem, 0)
-    copies += start_all(damp, sides_of(damp, (), 1), ssem, rsem, 12)
+    damps = start_all(damp, sides_of(damp, (), 1), ssem, rsem, 12)
     before, after = lax.rem(me + NDEV - 1, NDEV), lax.rem(me + 1, NDEV)
     rim = pltpu.make_async_remote_copy(
         src_ref=disp.at[:, 0:1, :], dst_ref=disp.at[:, NBLK:NBLK + 1, :], send_sem=ssem.at[32], recv_sem=rsem.at[32],
@@ -468,16 +515,21 @@
         shell_gather(q, disp, conn, dofs)
         blocks[q].wait()
         shell_product(q, stiff, dofs, force)
-    for cp in copies:
-        cp.wait()
-    for c in range(3):
-        clear_outside(vel.at[c])
 
     def pred_main(region):
         for c in range(3):
             predict(region, vel, c, pred)
 
-    all_planes(pred_main)
+    inner_planes(pred_main)
+    for cp in copies:
+        cp.wait()
+    pass_on(tokens.at[0], 2)
+    for c in range(3):
+        clear_outside(vel.at[c])
+
+    edge_planes(pred_main, 0)
+    for y in (OY, OY + CY - 1):
+        pred_main(Strip(y))
     for x in (OX - 1, OX + CX):
         for k in range(2):
             predict(Plane(x, OY + 16 * k, 16), vel, 0, pred)
@@ -498,13 +550,20 @@
     def swap(f, base):
         return start_all(f, corners_of(f, ()) + sides_of(f, (), 2), ssem, rsem, base)
 
-    def grow(f, before, out):
-        all_planes(lambda region: cheb(region, damp, f, before, out), OX - 1, OX + CX + 1)
-        for y in (OY - 1, OY + CY):
+    def grow_inner(f, before, out):
+        inner_planes(lambda region: cheb(region, damp, f, before, out))
+
+    def grow_edge(f, before, out):
+        edge_planes(lambda region: cheb(region, damp, f, before, out), 1)
+        for y in (OY - 1, OY, OY + CY - 1, OY + CY):
             cheb(Strip(y), damp, f, before, out)
         clear_outside(out)
 
     moving = swap(t0, 16)
+    pl.semaphore_wait(tokens.at[0], 2)
+    pass_on(tokens.at[1], 4)
+    for cp in damps:
+        cp.wait()
     rim.wait()
 
     @pl.when(me == NDEV - 1)
@@ -520,10 +579,13 @@
         device_id=(lax.div(after, NDOM), lax.rem(after, NDOM)), device_id_type=MESH)
     edge.start()
     shell_scatter(0, conn, force, own, over)
+    grow_inner(t0, None, t1)
     for cp in moving:
         cp.wait()
     clear_outside(t0)
-    grow(t0, None, t1)
+    pl.semaphore_wait(tokens.at[1], 2)
+    pass_on(tokens.at[2], 8)
+    grow_edge(t0, None, t1)
     all_planes(lambda region: cheb(region, damp, t1, t0, t2))
 
     moving = swap(t2, 24)
@@ -560,11 +622,12 @@
         place(W_BASIS + c, jnp.where(hit, WALL_FRICTION * ref[...], 0.0))
     basis_words(0, t0)
     basis_words(1, t1)
+    grow_inner(t2, t1, t3)
     for cp in moving:
         cp.wait()
     clear_outside(t2)
     basis_words(2, t2)
-    grow(t2, t1, t3)
+    grow_edge(t2, t1, t3)
 
     def dots(x, acc):
         acc = list(acc)
@@ -587,6 +650,7 @@
     payload = words[...]
     both = jnp.concatenate([payload, pltpu.roll(payload, W_NEXT, 1)], axis=0)
     rows_out[...] = pick(table[...], both) + row
+    pl.semaphore_wait(tokens.at[2], 2)
     mine = exchange_start(rows_out, rows_in, lsem.at[8], asem.at[0], asem.at[1])
     shell_scatter(1, conn, force, own, over)
     shell_scatter(2, conn, force, own, over)
@@ -738,6 +802,7 @@
             pltpu.SemaphoreType.DMA((34,)),
             pltpu.SemaphoreType.DMA((34,)),
             pltpu.SemaphoreType.DMA((4,)),
+            pltpu.SemaphoreType.REGULAR((3,)),
         ],
         compiler_params=pltpu.CompilerParams(
             collective_id=0, has_side_effects=True, vmem_limit_bytes=60 << 20),

time: 57 us -> 50.5 us (0.89)
  Pallas kernels: 54.6 us -> 48.1 us
    pallas_call x1, Pallas kernels: 52.1 us -> 45.6 us  [fused(): pl.pallas_call(step_kernel, out_shape=(jax.ShapeDtypeStruct(velocity.shap...]
where the time goes in v4:
time: 50.5 us; the launch traced here: 50.3 us
  Pallas kernels  48.1 us (95%)
  between operations  1.32 us (3%)
  local copies, waits for them, and re-layouts  0.64 us (1%)
    pallas_call x1, Pallas kernels, fused(): pl.pallas_call(step_kernel, out_shape=(jax.ShapeDtypeStruct(velocity.shap...  45.6 us
    pallas_call x1, Pallas kernels, relay(): pl.pallas_call(relay_kernel, out_shape=tuple((jax.ShapeDtypeStruct(a.shap...  2.51 us

profile of v4, /device:TPU:1, one launch (start us, length us, event | category | flops | bytes accessed | tf_op | source)
XLA Modules:
  0.0 50.3 jit_solution(4696422386098653102)
XLA Ops:
  0.6 0.0 copy-start
  0.6 0.0 copy-start.5
  0.7 0.0 copy-start.12
  0.7 0.0 copy-start.13
  0.7 0.0 copy-start.14
  0.7 45.6 %step.1 = (f32[3,16,32,256]{3,2,1,0:T(8,128)}, f32[16,32,256]{2,1,0:T(8,128)}, f32[3,4096]{1,0:T(4,128)}, f32[3,128]{1,0:T(4,128)}, s32[1,1]{1,0:T(1,128)}) custom-call(f32[3,16,32,256]{3,2,1,0:T(8,128)} %vel_hbm.1, f32[16,32,256]{2,1,0:T(8,128)} %damp_hbm.1, f32[12,12,4096]{2,1,0:T(8,128)} %stiff_hbm.1, f32[3,4096]{1,0:T(4,128)} %disp_in.1, ...), custom_call_target="tpu_custom_call" | custom-call | tf_op jit(solution)/shard_map/step/pallas_call | solution.py:768
  46.9 0.0 copy-done
  46.9 0.0 copy-done.5
  46.9 0.0 copy-done.12
  46.9 0.0 copy-done.13
  46.9 0.0 copy-done.14
  46.9 2.7 %conditional.1 = (f32[16,32,256]{2,1,0:T(8,128)}, f32[3,16,32,256]{3,2,1,0:T(8,128)}, f32[3,4096]{1,0:T(4,128)S(1)}, f32[3,128]{1,0:T(4,128)S(1)}) conditional(s32[]{:T(128)} %bitcast.64, (f32[3,16,32,256]{3,2,1,0:T(8,128)S(1)}, f32[16,32,256]{2,1,0:T(8,128)S(1)}, f32[4096]{0:T(1024)S(1)}, s32[128,1]{0,1:T(1,128)}, s32[128]{0:T(128)}, ...), branch_computations={%region_0.28_spmd, %region_28.29_spmd} | conditional | flops 47965312 | bytes 115600280 | solution.py:1030
  47.2 2.5 %relay.1 = (f32[3,16,32,256]{3,2,1,0:T(8,128)}, f32[4,4,32,256]{3,2,1,0:T(8,128)}, f32[3,4096]{1,0:T(4,128)S(1)}, f32[3,128]{1,0:T(4,128)S(1)}) custom-call(f32[3,16,32,256]{3,2,1,0:T(8,128)} %get-tuple-element.41.refs_0_, f32[4,4,32,256]{3,2,1,0:T(8,128)} %bitcast.105, f32[3,4096]{1,0:T(4,128)} %get-tuple-element.43.refs_2_, f32[3,128]{1,0:T(4,128)} %get-tuple-element.44.refs_3_), custom_call_target="tpu_custom_call" | custom-call | tf_op jit(solution)/shard_map/cond/branch_1_fun/relay/pallas_call | solution.py:1015
  49.7 0.0 copy-start.18
  49.7 0.0 copy-start.22
  49.7 0.6 %copy-done.18 = f32[3,4096]{1,0:T(4,128)} copy-done((f32[3,4096]{1,0:T(4,128)}, f32[3,4096]{1,0:T(4,128)S(1)}, u32[]{:S(2)}) %copy-start.18) | copy-done | bytes 49176
  50.3 0.0 copy-done.22
Async XLA Ops:
  0.6 46.3 %copy-start = (f32[3,16,32,256]{3,2,1,0:T(8,128)S(1)}, f32[3,16,32,256]{3,2,1,0:T(8,128)}, u32[]{:S(2)}) copy-start(f32[3,16,32,256]{3,2,1,0:T(8,128)} %vel_hbm.1) | copy-start | bytes 4718596
  0.6 46.3 %copy-start.5 = (f32[16,32,256]{2,1,0:T(8,128)S(1)}, f32[16,32,256]{2,1,0:T(8,128)}, u32[]{:S(2)}) copy-start(f32[16,32,256]{2,1,0:T(8,128)} %damp_hbm.1) | copy-start | bytes 1572868
  0.7 46.3 %copy-start.12 = (f32[3,4096]{1,0:T(4,128)S(1)}, f32[3,4096]{1,0:T(4,128)}, u32[]{:S(2)}) copy-start(f32[3,4096]{1,0:T(4,128)} %disp_in.1) | copy-start | bytes 147460
  0.7 46.3 %copy-start.13 = (s32[4,4096]{1,0:T(4,128)S(1)}, s32[4,4096]{1,0:T(4,128)}, u32[]{:S(2)}) copy-start(s32[4,4096]{1,0:T(4,128)} %conn_in.1) | copy-start | bytes 196612
  0.7 46.3 %copy-start.14 = (f32[4096]{0:T(1024)S(1)}, f32[4096]{0:T(1024)}, u32[]{:S(2)}) copy-start(f32[4096]{0:T(1024)} %param.18) | copy-start | bytes 49156
  49.7 0.6 %copy-start.18 = (f32[3,4096]{1,0:T(4,128)}, f32[3,4096]{1,0:T(4,128)S(1)}, u32[]{:S(2)}) copy-start(f32[3,4096]{1,0:T(4,128)S(1)} %get-tuple-element.180) | copy-start | bytes 147460
  49.7 0.6 %copy-start.22 = (f32[3,128]{1,0:T(4,128)}, f32[3,128]{1,0:T(4,128)S(1)}, u32[]{:S(2)}) copy-start(f32[3,128]{1,0:T(4,128)S(1)} %get-tuple-element.181) | copy-start | bytes 4612

commit v5 on v4

--- a/solution.py
+++ b/solution.py
@@ -17,7 +17,7 @@
 SHELL_STEP = 0.5
 RIM, RBFW, NBLK, NPTS = 64, 4, 32, 128
 W_BASIS, W_WEIGHT, W_NODE, W_NEXT = 32, 47, 51, 32
-PAIRS = [(i, j) for i in range(4) for j in range(i, 5)]
+EARLY, LATE = [(0, 0), (0, 1), (1, 1), (1, 2), (2, 2)], [(2, 3), (3, 3), (3, 4)]
 
 
 def rows_of(ref):
@@ -153,14 +153,10 @@
     lax.fori_loop(OX + 1, OX + CX - 1, body, 0, unroll=2)
 
 
-def edge_planes(fn, out):
-    def body(i, carry):
+def planes_at(fn, xs):
+    for x in xs:
         for k in range(2):
-            for base in (OX - out, OX + CX - 1):
-                fn(Plane(base + i, OY + k * (CY // 2), CY // 2))
-        return carry
-
-    lax.fori_loop(0, 1 + out, body, 0, unroll=1 + out)
+            fn(Plane(x, OY + k * (CY // 2), CY // 2))
 
 
 def position():
@@ -185,6 +181,27 @@
     @pl.when(d == NDOM - 1)
     def _():
         f[:, :, OY + CY:PY, :] = jnp.zeros((PX, 2, PY - OY - CY, HZ), jnp.float32)
+
+
+def clear_faces(f):
+    g, d = position()
+    xs, ys = slice(OX, OX + CX), slice(OY, OY + CY)
+
+    @pl.when(g == 0)
+    def _():
+        f[0:OX, :, ys, :] = jnp.zeros((OX, 2, CY, HZ), jnp.float32)
+
+    @pl.when(g == NGRP - 1)
+    def _():
+        f[OX + CX:PX, :, ys, :] = jnp.zeros((PX - OX - CX, 2, CY, HZ), jnp.float32)
+
+    @pl.when(d == 0)
+    def _():
+        f[xs, :, 0:OY, :] = jnp.zeros((CX, 2, OY, HZ), jnp.float32)
+
+    @pl.when(d == NDOM - 1)
+    def _():
+        f[xs, :, OY + CY:PY, :] = jnp.zeros((CX, 2, PY - OY - CY, HZ), jnp.float32)
 
 
 def neighbour(dg, dd):
@@ -469,8 +486,14 @@
     return jnp.sum(x, axis=1, keepdims=True)
 
 
-def step_kernel(vel_hbm, damp_hbm, stiff_hbm, disp_in, conn_in, mass, cells, cell_row, owner, node, weight, normal,
-                nv_hbm, p_hbm, disp_out, iface_out, flag_ref,
+def step_kernel(vel_hbm, damp_hbm, stiff_hbm, disp_hbm, conn_hbm, *rest):
+    small_hbm, rest = rest[:7], rest[7:]
+    small, rest = rest[-7:], rest[:-7]
+    step_body(vel_hbm, damp_hbm, stiff_hbm, disp_hbm, conn_hbm, small_hbm, small, *rest)
+
+
+def step_body(vel_hbm, damp_hbm, stiff_hbm, disp_hbm, conn_hbm, small_hbm, small,
+                nv_hbm, p_hbm, disp_res, iface_res, flag_ref, disp_in, conn_in, disp_out, iface_out, msem,
                 vel, damp, pred, t0, t1, t2, t3, press, nvel, stiff,
                 disp, conn, dofs, force, own, over, mid0, mid1, dx, dy, words, table, nodal,
                 rows_out, rows_in, back_out, back_in, lsem, ksem, ssem, rsem, asem, tokens):
@@ -488,12 +511,13 @@
     for q in range(4):
         z = slice(q * 8 * HZ, (q + 1) * 8 * HZ)
         loads.append(pltpu.make_async_copy(stiff_hbm.at[:, :, z], stiff.at[:, :, z], ksem.at[q]))
-    for cp in loads:
+    minor = [pltpu.make_async_copy(a, b, msem.at[n])
+             for n, (a, b) in enumerate(zip((disp_hbm, conn_hbm) + small_hbm, (disp_in, conn_in) + small))]
+    for cp in loads[:8] + minor + loads[8:]:
         cp.start()
     blocks = loads[8:]
-
-    spread(disp_in, disp.reshape(3 * 40, HZ), 3, 40)
-    spread(conn_in, conn.reshape(4 * NBLK, HZ), 4, NBLK)
+    mass, cells, cell_row, owner, node, weight, normal = small
+
     square = (HZ, HZ)
     for cp in loads[:8]:
         cp.wait()
@@ -506,11 +530,15 @@
     thin_x, thin_y = sides_of(vel, (slice(1, 3),), 1)[:2], sides_of(vel, (slice(0, 2),), 1)[2:]
     copies = start_all(vel, faces + wide_x + wide_y + thin_x + thin_y, ssem, rsem, 0)
     damps = start_all(damp, sides_of(damp, (), 1), ssem, rsem, 12)
+    minor[0].wait()
+    spread(disp_in, disp.reshape(3 * 40, HZ), 3, 40)
     before, after = lax.rem(me + NDEV - 1, NDEV), lax.rem(me + 1, NDEV)
     rim = pltpu.make_async_remote_copy(
         src_ref=disp.at[:, 0:1, :], dst_ref=disp.at[:, NBLK:NBLK + 1, :], send_sem=ssem.at[32], recv_sem=rsem.at[32],
         device_id=(lax.div(before, NDOM), lax.rem(before, NDOM)), device_id_type=MESH)
     rim.start()
+    minor[1].wait()
+    spread(conn_in, conn.reshape(4 * NBLK, HZ), 4, NBLK)
     for q in range(3):
         shell_gather(q, disp, conn, dofs)
         blocks[q].wait()
@@ -521,18 +549,19 @@
             predict(region, vel, c, pred)
 
     inner_planes(pred_main)
-    for cp in copies:
+    for cp in copies[4:]:
+        cp.wait()
+    for c in range(3):
+        clear_faces(vel.at[c])
+    planes_at(pred_main, (OX, OX + CX - 1))
+    for y in (OY, OY + CY - 1):
+        pred_main(Strip(y))
+    for cp in copies[:4]:
         cp.wait()
     pass_on(tokens.at[0], 2)
-    for c in range(3):
-        clear_outside(vel.at[c])
-
-    edge_planes(pred_main, 0)
-    for y in (OY, OY + CY - 1):
-        pred_main(Strip(y))
-    for x in (OX - 1, OX + CX):
-        for k in range(2):
-            predict(Plane(x, OY + 16 * k, 16), vel, 0, pred)
+    for c in (0, 1):
+        clear_outside(vel.at[SLOT[c]])
+    planes_at(lambda region: predict(region, vel, 0, pred), (OX - 1, OX + CX))
     for y in (OY - 1, OY + CY):
         predict(Strip(y), vel, 1, pred)
     clear_outside(pred.at[f_x])
@@ -553,10 +582,20 @@
     def grow_inner(f, before, out):
         inner_planes(lambda region: cheb(region, damp, f, before, out))
 
-    def grow_edge(f, before, out):
-        edge_planes(lambda region: cheb(region, damp, f, before, out), 1)
-        for y in (OY - 1, OY, OY + CY - 1, OY + CY):
-            cheb(Strip(y), damp, f, before, out)
+    def grow_edge(moving, f, before, out):
+        for cp in moving[4:]:
+            cp.wait()
+        clear_faces(f)
+        grow = lambda region: cheb(region, damp, f, before, out)
+        planes_at(grow, (OX, OX + CX - 1))
+        for y in (OY, OY + CY - 1):
+            grow(Strip(y))
+        for cp in moving[:4]:
+            cp.wait()
+        clear_outside(f)
+        planes_at(grow, (OX - 1, OX + CX))
+        for y in (OY - 1, OY + CY):
+            grow(Strip(y))
         clear_outside(out)
 
     moving = swap(t0, 16)
@@ -580,15 +619,14 @@
     edge.start()
     shell_scatter(0, conn, force, own, over)
     grow_inner(t0, None, t1)
-    for cp in moving:
-        cp.wait()
-    clear_outside(t0)
     pl.semaphore_wait(tokens.at[1], 2)
     pass_on(tokens.at[2], 8)
-    grow_edge(t0, None, t1)
+    grow_edge(moving, t0, None, t1)
     all_planes(lambda region: cheb(region, damp, t1, t0, t2))
 
     moving = swap(t2, 24)
+    for cp in minor[2:]:
+        cp.wait()
     owns = owner[...] == row_of(square)
     first = jnp.min(jnp.where(owns, lane_of(square), HZ), axis=1, keepdims=True)
     for s in (0, 1):
@@ -604,6 +642,22 @@
     hit = hit0 | hit1
     normals = [column(normal[c:c + 1, :]) for c in range(3)]
 
+    lane1 = lane_of((1, HZ))
+
+    def gather_dots(pairs, fields):
+        def body(x, acc):
+            acc = list(acc)
+            for k in range(2):
+                ts = fields(Plane(x, OY + 16 * k, 16))
+                for n, (i, j) in enumerate(pairs):
+                    for h in (0, 1):
+                        prod = ts[i][h] * ts[j][h]
+                        acc[n] = acc[n] + (prod[0:8] + prod[8:16])
+            return tuple(acc)
+
+        acc = lax.fori_loop(OX, OX + CX, body, tuple(jnp.zeros((8, HZ), jnp.float32) for _ in pairs), unroll=2)
+        return [total_of(jnp.sum(a, axis=0, keepdims=True)) for a in acc]
+
     def place(word, values):
         words[...] += jnp.where(lane == word, total_of(values), 0.0)
 
@@ -623,30 +677,16 @@
     basis_words(0, t0)
     basis_words(1, t1)
     grow_inner(t2, t1, t3)
-    for cp in moving:
-        cp.wait()
-    clear_outside(t2)
+    early = gather_dots(EARLY, lambda region: [region.get(t) for t in (t0, t1, t2)])
+    row = jnp.zeros((1, HZ), jnp.float32)
+    for n, part in enumerate(early):
+        row = row + jnp.where(lane1 == n, part, 0.0)
+    grow_edge(moving, t2, t1, t3)
     basis_words(2, t2)
-    grow_edge(t2, t1, t3)
-
-    def dots(x, acc):
-        acc = list(acc)
-        for k in range(2):
-            region = Plane(x, OY + 16 * k, 16)
-            ts = [region.get(t) for t in (t0, t1, t2, t3)]
-            ts.append(cheb(region, damp, t3, t2, None))
-            for n, (i, j) in enumerate(PAIRS):
-                for h in (0, 1):
-                    prod = ts[i][h] * ts[j][h]
-                    acc[n] = acc[n] + (prod[0:8] + prod[8:16])
-        return tuple(acc)
-
-    acc = lax.fori_loop(OX, OX + CX, dots, tuple(jnp.zeros((8, HZ), jnp.float32) for _ in PAIRS))
+    late = gather_dots(LATE, lambda region: [None, None, region.get(t2), region.get(t3), cheb(region, damp, t3, t2, None)])
     basis_words(3, t3)
-    lane1 = lane_of((1, HZ))
-    row = jnp.zeros((1, HZ), jnp.float32)
-    for n in range(len(PAIRS)):
-        row = row + jnp.where(lane1 == n, total_of(jnp.sum(acc[n], axis=0, keepdims=True)), 0.0)
+    for n, part in enumerate(late):
+        row = row + jnp.where(lane1 == len(EARLY) + n, part, 0.0)
     payload = words[...]
     both = jnp.concatenate([payload, pltpu.roll(payload, W_NEXT, 1)], axis=0)
     rows_out[...] = pick(table[...], both) + row
@@ -663,9 +703,11 @@
     exchange_wait(mine, rows_out, rows_in, asem.at[0], asem.at[1])
     got = rows_in[...]
     total = jnp.sum(got, axis=0, keepdims=True)
-    gram = {}
-    for n, key in enumerate(PAIRS):
-        gram[key] = jnp.broadcast_to(total_of(jnp.where(lane1 == n, total, 0.0)), (1, HZ))
+    sums = [jnp.broadcast_to(total_of(jnp.where(lane1 == n, total, 0.0)), (1, HZ)) for n in range(8)]
+    moment = list(sums[:2])
+    for k in range(2, 8):
+        moment.append(2.0 * sums[k] - moment[k % 2])
+    gram = {(i, j): 0.5 * (moment[i + j] + moment[j - i]) for i in range(5) for j in range(i, 5) if i + j < 8}
     coef, worst = iterate(lambda i, j: gram[(i, j)])
     flag_ref[0, 0] = jnp.where(worst > GUARD, 1, 0).astype(jnp.int32)[0, 0]
 
@@ -747,12 +789,16 @@
         cp.start()
     for b in range(NBLK):
         disp_out[:, b * HZ:(b + 1) * HZ] = force.reshape(12 * NBLK, HZ)[pl.ds(b, 3, stride=NBLK), :]
+    stores.append(pltpu.make_async_copy(disp_out, disp_res, lsem.at[4]))
+    stores[-1].start()
     exchange_wait(mine, back_out, back_in, asem.at[2], asem.at[3])
     answers = jnp.transpose(back_in[...])[0:8]
     answers = jnp.concatenate(thirds(answers), axis=0)
     found = [jnp.dot(answers, table[:, s * HZ:(s + 1) * HZ], preferred_element_type=jnp.float32) for s in (0, 1)]
     found = [f[0:8] + f[8:16] + f[16:24] for f in found]
     iface_out[...] = found[0][0:3] + found[1][3:6]
+    stores.append(pltpu.make_async_copy(iface_out, iface_res, lsem.at[5]))
+    stores[-1].start()
     for cp in stores:
         cp.wait()
 
@@ -762,7 +808,6 @@
     field = (PX, 2, PY, HZ)
     f32, i32 = jnp.float32, jnp.int32
     anywhere = pl.BlockSpec(memory_space=pl.ANY)
-    vmem = pl.BlockSpec(memory_space=pltpu.VMEM)
     smem = pl.BlockSpec(memory_space=pltpu.SMEM)
     square = pltpu.VMEM((HZ, HZ), f32)
     outs = pl.pallas_call(
@@ -774,9 +819,14 @@
             jax.ShapeDtypeStruct(normals.shape, f32),
             jax.ShapeDtypeStruct((1, 1), i32),
         ),
-        in_specs=[anywhere] * 3 + [vmem] * 3 + [smem] + [vmem] * 5,
-        out_specs=(anywhere, anywhere, vmem, vmem, smem),
+        in_specs=[pl.BlockSpec(memory_space=pltpu.HBM)] * 12,
+        out_specs=(anywhere,) * 4 + (smem,),
         scratch_shapes=[
+            pltpu.VMEM(displacement.shape, f32),
+            pltpu.VMEM(connectivity.shape, i32),
+            pltpu.VMEM(displacement.shape, f32),
+            pltpu.VMEM(normals.shape, f32),
+            pltpu.SemaphoreType.DMA((9,)),
             pltpu.VMEM((3,) + field, f32),
             pltpu.VMEM(field, f32),
             pltpu.VMEM((3,) + field, f32),
@@ -803,9 +853,16 @@
             pltpu.SemaphoreType.DMA((34,)),
             pltpu.SemaphoreType.DMA((4,)),
             pltpu.SemaphoreType.REGULAR((3,)),
+            pltpu.VMEM((NBLK, HZ), f32),
+            pltpu.SMEM((NPTS,), i32),
+            pltpu.VMEM((1, NPTS), i32),
+            pltpu.VMEM((1, NPTS), i32),
+            pltpu.VMEM((1, NPTS), i32),
+            pltpu.VMEM((RBFW, NPTS), f32),
+            pltpu.VMEM((3, NPTS), f32),
         ],
         compiler_params=pltpu.CompilerParams(
-            collective_id=0, has_side_effects=True, vmem_limit_bytes=60 << 20),
+            collective_id=0, has_side_effects=True, vmem_limit_bytes=VLIMIT << 20),
         name="step",
     )(
         velocity, damping, stiffness, displacement, connectivity, inv_mass.reshape(NBLK, HZ), iface_cell,
@@ -817,6 +874,7 @@
 ITERS = 4
 VISCOSITY = 1.0
 GUARD = 4e-4
+VLIMIT = 60
 UNIT_STEPS = ((1, 0, 0), (0, 1, 0), (0, 0, 1))
 
 

time: 50.5 us -> 49.1 us (0.972)
  Pallas kernels: 48.1 us -> 46.8 us
    pallas_call x1, Pallas kernels: 45.6 us -> 44.3 us  [fused(): pl.pallas_call(step_kernel, out_shape=(jax.ShapeDtypeStruct(velocity.shap...]
where the time goes in v5:
time: 49.1 us; the launch traced here: 49 us
  Pallas kernels  46.8 us (95%)
  between operations  1.32 us (3%)
  local copies, waits for them, and re-layouts  0.64 us (1%)
    pallas_call x1, Pallas kernels, fused(): pl.pallas_call(step_kernel, out_shape=(jax.ShapeDtypeStruct(velocity.shap...  44.3 us
    pallas_call x1, Pallas kernels, relay(): pl.pallas_call(relay_kernel, out_shape=tuple((jax.ShapeDtypeStruct(a.shap...  2.51 us

profile of v5, /device:TPU:1, one launch (start us, length us, event | category | flops | bytes accessed | tf_op | source)
XLA Modules:
  0.0 49.0 jit_solution(7784764456699476054)
XLA Ops:
  0.6 0.0 copy-start
  0.6 0.0 copy-start.5
  0.7 0.0 copy-start.12
  0.7 0.0 copy-start.13
  0.7 0.0 copy-start.14
  0.7 44.3 %step.1 = (f32[3,16,32,256]{3,2,1,0:T(8,128)}, f32[16,32,256]{2,1,0:T(8,128)}, f32[3,4096]{1,0:T(4,128)}, f32[3,128]{1,0:T(4,128)}, s32[1,1]{1,0:T(1,128)}) custom-call(f32[3,16,32,256]{3,2,1,0:T(8,128)} %vel_hbm.1, f32[16,32,256]{2,1,0:T(8,128)} %damp_hbm.1, f32[12,12,4096]{2,1,0:T(8,128)} %stiff_hbm.1, f32[3,4096]{1,0:T(4,128)} %disp_hbm.1, ...), custom_call_target="tpu_custom_call" | custom-call | tf_op jit(solution)/shard_map/step/pallas_call | solution.py:813
  45.5 0.0 copy-done
  45.5 0.0 copy-done.5
  45.6 0.0 copy-done.12
  45.6 0.0 copy-done.13
  45.6 0.0 copy-done.14
  45.6 2.7 %conditional.1 = (f32[16,32,256]{2,1,0:T(8,128)}, f32[3,16,32,256]{3,2,1,0:T(8,128)}, f32[3,4096]{1,0:T(4,128)S(1)}, f32[3,128]{1,0:T(4,128)S(1)}) conditional(s32[]{:T(128)} %bitcast.64, (f32[3,16,32,256]{3,2,1,0:T(8,128)S(1)}, f32[16,32,256]{2,1,0:T(8,128)S(1)}, f32[4096]{0:T(1024)S(1)}, s32[128,1]{0,1:T(1,128)}, s32[128]{0:T(128)}, ...), branch_computations={%region_0.28_spmd, %region_28.29_spmd} | conditional | flops 47965312 | bytes 115600280 | solution.py:1088
  45.8 2.5 %relay.1 = (f32[3,16,32,256]{3,2,1,0:T(8,128)}, f32[4,4,32,256]{3,2,1,0:T(8,128)}, f32[3,4096]{1,0:T(4,128)S(1)}, f32[3,128]{1,0:T(4,128)S(1)}) custom-call(f32[3,16,32,256]{3,2,1,0:T(8,128)} %get-tuple-element.41.refs_0_, f32[4,4,32,256]{3,2,1,0:T(8,128)} %bitcast.105, f32[3,4096]{1,0:T(4,128)} %get-tuple-element.43.refs_2_, f32[3,128]{1,0:T(4,128)} %get-tuple-element.44.refs_3_), custom_call_target="tpu_custom_call" | custom-call | tf_op jit(solution)/shard_map/cond/branch_1_fun/relay/pallas_call | solution.py:1073
  48.3 0.0 copy-start.18
  48.4 0.0 copy-start.22
  48.4 0.6 %copy-done.18 = f32[3,4096]{1,0:T(4,128)} copy-done((f32[3,4096]{1,0:T(4,128)}, f32[3,4096]{1,0:T(4,128)S(1)}, u32[]{:S(2)}) %copy-start.18) | copy-done | bytes 49176
  49.0 0.0 copy-done.22
Async XLA Ops:
  0.6 44.9 %copy-start = (f32[3,16,32,256]{3,2,1,0:T(8,128)S(1)}, f32[3,16,32,256]{3,2,1,0:T(8,128)}, u32[]{:S(2)}) copy-start(f32[3,16,32,256]{3,2,1,0:T(8,128)} %vel_hbm.1) | copy-start | bytes 4718596
  0.6 44.9 %copy-start.5 = (f32[16,32,256]{2,1,0:T(8,128)S(1)}, f32[16,32,256]{2,1,0:T(8,128)}, u32[]{:S(2)}) copy-start(f32[16,32,256]{2,1,0:T(8,128)} %damp_hbm.1) | copy-start | bytes 1572868
  0.7 44.9 %copy-start.12 = (f32[3,4096]{1,0:T(4,128)S(1)}, f32[3,4096]{1,0:T(4,128)}, u32[]{:S(2)}) copy-start(f32[3,4096]{1,0:T(4,128)} %disp_hbm.1) | copy-start | bytes 147460
  0.7 44.9 %copy-start.13 = (s32[4,4096]{1,0:T(4,128)S(1)}, s32[4,4096]{1,0:T(4,128)}, u32[]{:S(2)}) copy-start(s32[4,4096]{1,0:T(4,128)} %conn_hbm.1) | copy-start | bytes 196612
  0.7 44.9 %copy-start.14 = (f32[4096]{0:T(1024)S(1)}, f32[4096]{0:T(1024)}, u32[]{:S(2)}) copy-start(f32[4096]{0:T(1024)} %param.18) | copy-start | bytes 49156
  48.3 0.6 %copy-start.18 = (f32[3,4096]{1,0:T(4,128)}, f32[3,4096]{1,0:T(4,128)S(1)}, u32[]{:S(2)}) copy-start(f32[3,4096]{1,0:T(4,128)S(1)} %get-tuple-element.180) | copy-start | bytes 147460
  48.4 0.6 %copy-start.22 = (f32[3,128]{1,0:T(4,128)}, f32[3,128]{1,0:T(4,128)S(1)}, u32[]{:S(2)}) copy-start(f32[3,128]{1,0:T(4,128)S(1)} %get-tuple-element.181) | copy-start | bytes 4612

commit v6 on v5

--- a/solution.py
+++ b/solution.py
@@ -451,8 +451,8 @@
 
 def sample(cells, f, mid0, mid1, dx, dy):
     def body(i, carry):
-        for u in range(4):
-            k = i * 4 + u
+        for u in range(8):
+            k = i * 8 + u
             cell = cells[k]
             x, y, h = (cell >> 13) + OX, ((cell >> 8) & (CY - 1)) + OY, (cell >> 7) & 1
             at = pl.ds(k, 1)
@@ -462,20 +462,20 @@
             dy[at, :] = f[x, h, pl.ds(y + 1, 1), :] - f[x, h, pl.ds(y - 1, 1), :]
         return carry
 
-    lax.fori_loop(0, NPTS // 4, body, 0)
+    lax.fori_loop(0, NPTS // 8, body, 0)
 
 
 def sample_centre(cells, fields, outs):
     def body(i, carry):
-        for u in range(4):
-            k = i * 4 + u
+        for u in range(8):
+            k = i * 8 + u
             cell = cells[k]
             x, y, h = (cell >> 13) + OX, ((cell >> 8) & (CY - 1)) + OY, (cell >> 7) & 1
             for f, o in zip(fields, outs):
                 o[pl.ds(k, 1), :] = f[x, h, pl.ds(y, 1), :]
         return carry
 
-    lax.fori_loop(0, NPTS // 4, body, 0)
+    lax.fori_loop(0, NPTS // 8, body, 0)
 
 
 def column(row):
@@ -1074,7 +1074,7 @@
         relay_kernel,
         out_shape=tuple(jax.ShapeDtypeStruct(a.shape, a.dtype) for a in arrays),
         in_specs=[anywhere] * len(arrays),
-        out_specs=(anywhere,) * len(arrays),
+        out_specs=(pl.BlockSpec(memory_space=pltpu.HBM),) * len(arrays),
         scratch_shapes=[pltpu.VMEM(a.shape, a.dtype) for a in arrays]
         + [pltpu.SemaphoreType.DMA((count,)), pltpu.SemaphoreType.DMA((count,))],
         compiler_params=pltpu.CompilerParams(vmem_limit_bytes=60 << 20),

time: 49.1 us -> 49 us (level)
  no operation moved by 1% of the time
where the time goes in v6:
time: 49 us; the launch traced here: 48.8 us
  Pallas kernels  46.6 us (95%)
  between operations  1.32 us (3%)
  local copies, waits for them, and re-layouts  0.64 us (1%)
    pallas_call x1, Pallas kernels, fused(): pl.pallas_call(step_kernel, out_shape=(jax.ShapeDtypeStruct(velocity.shap...  44.1 us
    pallas_call x1, Pallas kernels, relay(): pl.pallas_call(relay_kernel, out_shape=tuple((jax.ShapeDtypeStruct(a.shap...  2.51 us

profile of v6, /device:TPU:1, one launch (start us, length us, event | category | flops | bytes accessed | tf_op | source)
XLA Modules:
  0.0 48.8 jit_solution(10125279000485735305)
XLA Ops:
  0.6 0.0 copy-start
  0.6 0.0 copy-start.5
  0.7 0.0 copy-start.12
  0.7 0.0 copy-start.13
  0.7 0.0 copy-start.14
  0.7 44.1 %step.1 = (f32[3,16,32,256]{3,2,1,0:T(8,128)}, f32[16,32,256]{2,1,0:T(8,128)}, f32[3,4096]{1,0:T(4,128)}, f32[3,128]{1,0:T(4,128)}, s32[1,1]{1,0:T(1,128)}) custom-call(f32[3,16,32,256]{3,2,1,0:T(8,128)} %vel_hbm.1, f32[16,32,256]{2,1,0:T(8,128)} %damp_hbm.1, f32[12,12,4096]{2,1,0:T(8,128)} %stiff_hbm.1, f32[3,4096]{1,0:T(4,128)} %disp_hbm.1, ...), custom_call_target="tpu_custom_call" | custom-call | tf_op jit(solution)/shard_map/step/pallas_call | solution.py:813
  45.4 0.0 copy-done
  45.4 0.0 copy-done.5
  45.4 0.0 copy-done.12
  45.4 0.0 copy-done.13
  45.4 0.0 copy-done.14
  45.4 2.7 %conditional.1 = (f32[16,32,256]{2,1,0:T(8,128)}, f32[3,16,32,256]{3,2,1,0:T(8,128)}, f32[3,4096]{1,0:T(4,128)S(1)}, f32[3,128]{1,0:T(4,128)S(1)}) conditional(s32[]{:T(128)} %bitcast.64, (f32[3,16,32,256]{3,2,1,0:T(8,128)S(1)}, f32[16,32,256]{2,1,0:T(8,128)S(1)}, f32[4096]{0:T(1024)S(1)}, s32[128,1]{0,1:T(1,128)}, s32[128]{0:T(128)}, ...), branch_computations={%region_0.28_spmd, %region_28.29_spmd} | conditional | flops 47965312 | bytes 115600280 | solution.py:1088
  45.7 2.5 %relay.1 = (f32[3,16,32,256]{3,2,1,0:T(8,128)}, f32[4,4,32,256]{3,2,1,0:T(8,128)}, f32[3,4096]{1,0:T(4,128)S(1)}, f32[3,128]{1,0:T(4,128)S(1)}) custom-call(f32[3,16,32,256]{3,2,1,0:T(8,128)} %get-tuple-element.41.refs_0_, f32[4,4,32,256]{3,2,1,0:T(8,128)} %bitcast.105, f32[3,4096]{1,0:T(4,128)} %get-tuple-element.43.refs_2_, f32[3,128]{1,0:T(4,128)} %get-tuple-element.44.refs_3_), custom_call_target="tpu_custom_call" | custom-call | tf_op jit(solution)/shard_map/cond/branch_1_fun/relay/pallas_call | solution.py:1073
  48.2 0.0 copy-start.18
  48.2 0.0 copy-start.22
  48.2 0.6 %copy-done.18 = f32[3,4096]{1,0:T(4,128)} copy-done((f32[3,4096]{1,0:T(4,128)}, f32[3,4096]{1,0:T(4,128)S(1)}, u32[]{:S(2)}) %copy-start.18) | copy-done | bytes 49176
  48.8 0.0 copy-done.22
Async XLA Ops:
  0.6 44.7 %copy-start = (f32[3,16,32,256]{3,2,1,0:T(8,128)S(1)}, f32[3,16,32,256]{3,2,1,0:T(8,128)}, u32[]{:S(2)}) copy-start(f32[3,16,32,256]{3,2,1,0:T(8,128)} %vel_hbm.1) | copy-start | bytes 4718596
  0.6 44.7 %copy-start.5 = (f32[16,32,256]{2,1,0:T(8,128)S(1)}, f32[16,32,256]{2,1,0:T(8,128)}, u32[]{:S(2)}) copy-start(f32[16,32,256]{2,1,0:T(8,128)} %damp_hbm.1) | copy-start | bytes 1572868
  0.7 44.7 %copy-start.12 = (f32[3,4096]{1,0:T(4,128)S(1)}, f32[3,4096]{1,0:T(4,128)}, u32[]{:S(2)}) copy-start(f32[3,4096]{1,0:T(4,128)} %disp_hbm.1) | copy-start | bytes 147460
  0.7 44.7 %copy-start.13 = (s32[4,4096]{1,0:T(4,128)S(1)}, s32[4,4096]{1,0:T(4,128)}, u32[]{:S(2)}) copy-start(s32[4,4096]{1,0:T(4,128)} %conn_hbm.1) | copy-start | bytes 196612
  0.7 44.7 %copy-start.14 = (f32[4096]{0:T(1024)S(1)}, f32[4096]{0:T(1024)}, u32[]{:S(2)}) copy-start(f32[4096]{0:T(1024)} %param.18) | copy-start | bytes 49156
  48.2 0.6 %copy-start.18 = (f32[3,4096]{1,0:T(4,128)}, f32[3,4096]{1,0:T(4,128)S(1)}, u32[]{:S(2)}) copy-start(f32[3,4096]{1,0:T(4,128)S(1)} %get-tuple-element.180) | copy-start | bytes 147460
  48.2 0.6 %copy-start.22 = (f32[3,128]{1,0:T(4,128)}, f32[3,128]{1,0:T(4,128)S(1)}, u32[]{:S(2)}) copy-start(f32[3,128]{1,0:T(4,128)S(1)} %get-tuple-element.181) | copy-start | bytes 4612
